TPU v7x, 32 devices: a whole 2x2x4 slice. The times are simulated.
32 devices in a mesh: lat: 4 (over y, core), lon: 8 (over z, x).
Axes of the slice: x: 2, y: 2, z: 4, core: 2. Of those that a mesh axis runs over, the one named last changes fastest.
Arguments:
- tracers: float32 [2, 4, 64, 2048], P(None, None, 'lat', 'lon'), may hold values from -6 to 6
- cotangent: float32 [2, 4, 64, 2048], P(None, None, 'lat', 'lon'), may hold values from -6 to 6
- land_mask: int32 [4, 64, 2048], P(None, 'lat', 'lon'), may hold values 0 or 1
- diffusion: float32 [3, 4, 64, 2048], P(None, None, 'lat', 'lon'), may hold values from 0.01 to 0.1
- velocity: float32 [2, 4, 64, 2048], P(None, None, 'lat', 'lon'), may hold values from -0.1 to 0.1
- weights: float32 [32, 128, 128], replicated, may hold values from -0.1875 to 0.1875
- atm_state: float32 [2, 4, 2048, 128], P(None, 'lat', 'lon'), may hold values from -6 to 6
- margins: int32 [3, 4, 8, 8, 64], P(None, 'lat', 'lon'), may hold values from -1 to 255, as said below
Outputs:
- final_tracers: float32 [2, 4, 64, 2048], P(None, None, 'lat', 'lon')
- adjoint_tracers: float32 [2, 4, 64, 2048], P(None, None, 'lat', 'lon')
- atm_gradient: float32 [2, 4, 2048, 128], P(None, 'lat', 'lon')
Inputs may be any that keep to these rules, and one draw needn't show every extreme that they name: margins[0, i, j, k, s] is a top-level block of ocean tile (i, k), or -1 where slot s from longitude tile j to longitude tile k in latitude row i is empty; margins[1] is an atmosphere block of tile (i, j) and margins[2] a weight block in every slot. Live slots lie anywhere among the 64. In each latitude row one receiving tile has all 64 slots live from every sender.
All inputs are finite; a program needn't handle non-finite values. No bound on the sum of `land_mask` on one device may be relied on, other than what follows from the above.
Results may differ from a plain program's by a relative error of at most 0.0003.
Values sent between devices are 32-bit elements; how exact they have to be, the bound alone decides.
No kernel may reach another device: no remote copies, remote signals or barrier semaphores. Data moves between devices by JAX's collectives and lax.ppermute only.
A program may use at most 64 MiB of HBM per device.

v0:
```python
import functools

import jax
import jax.numpy as jnp
from jax import lax
from jax.experimental import pallas as pl
from jax.experimental.pallas import tpu as pltpu
from jax.sharding import PartitionSpec as P

BLOCK = 128
STEPS = 4
HALO = STEPS
PER_LANES = BLOCK // HALO
GROUP = 4
f32 = jnp.float32
bf16 = jnp.bfloat16
VMEM_LIMIT = 48 * 1024 * 1024


def call(body, outs, scratch=(), flops=0, name=None, inputs=0, far=()):
    outs = [s if isinstance(s, jax.ShapeDtypeStruct) else jax.ShapeDtypeStruct(s, f32) for s in outs]
    near = pl.BlockSpec(memory_space=pltpu.VMEM)
    kernel = pl.pallas_call(
        body,
        out_shape=outs,
        in_specs=[pl.BlockSpec(memory_space=pltpu.HBM) if n in far else near for n in range(inputs)],
        out_specs=[near] * len(outs),
        scratch_shapes=list(scratch),
        compiler_params=pltpu.CompilerParams(vmem_limit_bytes=VMEM_LIMIT),
        cost_estimate=pl.CostEstimate(flops=flops, bytes_accessed=1 << 20, transcendentals=0),
        name=name,
    )

    def run(*args):
        return kernel(
            *(pltpu.with_memory_space_constraint(x, pltpu.HBM) if n in far else x for n, x in enumerate(args))
        )

    return run


def lanes(shape):
    return lax.broadcasted_iota(jnp.int32, shape, len(shape) - 1)


def rows(shape):
    return lax.broadcasted_iota(jnp.int32, shape, len(shape) - 2)


def turn(x, shift, axis):
    shift %= x.shape[axis]
    return pltpu.roll(x, shift, axis) if shift else x


def tile_fields(tracers, cotangent, land_mask, diffusion, velocity):
    levels = land_mask.shape[0]
    mask = [land_mask[level].astype(f32) for level in range(levels)]
    out = [tracers[f, level] for f in range(2) for level in range(levels)]
    out += [cotangent[f, level] for f in range(2) for level in range(levels)]
    out += [diffusion[0, level] * mask[level] for level in range(levels)]
    out += [velocity[0, level] * mask[level] for level in range(levels)]
    out += [diffusion[1, level] * mask[level] for level in range(levels)]
    out += [velocity[1, level] * mask[level] for level in range(levels)]
    out += [diffusion[2, level] * mask[level] * mask[level + 1] for level in range(levels - 1)]
    return out


def fetch(pairs, arrived):
    copies = [pltpu.make_async_copy(src, dst, arrived.at[n]) for n, (src, dst) in enumerate(pairs)]
    for copy in copies:
        copy.start()
    return copies


def pack_columns(*refs):
    inputs, (fields, to_west, to_east), scratch = refs[:5], refs[5:8], refs[8:]
    for copy in fetch(zip(inputs, scratch[:5]), scratch[5]):
        copy.wait()
    shape = to_west.shape[1:]
    lane = lanes(shape)
    west = [jnp.zeros(shape, f32) for _ in range(to_west.shape[0])]
    east = [jnp.zeros(shape, f32) for _ in range(to_west.shape[0])]
    for i, field in enumerate(tile_fields(*scratch[:5])):
        fields[i] = field
        part, at = divmod(i, PER_LANES)
        at *= HALO
        here = (lane >= at) & (lane < at + HALO)
        west[part] = jnp.where(here, turn(field[:, :BLOCK], at, 1), west[part])
        east[part] = jnp.where(here, turn(field[:, -BLOCK:], at + HALO, 1), east[part])
    for part in range(to_west.shape[0]):
        to_west[part] = west[part]
        to_east[part] = east[part]


def unpack_columns(from_west, from_east, i):
    part, at = divmod(i, PER_LANES)
    at *= HALO
    lane = lanes(from_west[part].shape)
    east = turn(from_east[part], -at, 1)
    west = turn(from_west[part], -at - HALO, 1)
    return jnp.where(lane < HALO, east, jnp.where(lane >= BLOCK - HALO, west, 0.0))


def row_sources(fields, from_west, from_east, sums):
    out = [(fields, (i, slice(None), slice(h * BLOCK, (h + 1) * BLOCK)))
           for i in range(fields.shape[0]) for h in range(fields.shape[2] // BLOCK)]
    for columns in (from_west, from_east):
        out += [(columns, (part,)) for part in range(columns.shape[0])]
    return out + [(sums, (k, part)) for k in range(sums.shape[0]) for part in range(sums.shape[1])]


def pack_rows(fields, from_west, from_east, sums, to_north, to_south):
    sources = [ref[at] for ref, at in row_sources(fields, from_west, from_east, sums)]
    half = to_north.shape[0]
    row = rows((8, BLOCK))
    for i in range(half):
        first = sources[i]
        second = sources[i + half] if i + half < len(sources) else jnp.zeros_like(first)
        to_north[i] = jnp.where(row < HALO, turn(first[-8:], HALO, 0), second[-8:])
        to_south[i] = jnp.where(row < HALO, first[:8], turn(second[:8], HALO, 0))


def edge_rows(from_north, from_south, i):
    half = from_north.shape[0]
    if i < half:
        north, south = from_north[i], turn(from_south[i], HALO, 0)
    else:
        north, south = turn(from_north[i - half], HALO, 0), from_south[i - half]
    return jnp.where(rows((8, BLOCK)) < HALO, north, south)


def widen(fields, from_west, from_east, from_north, from_south, wide):
    count, tile_lat, tile_lon = fields.shape
    halves = tile_lon // BLOCK
    parts = from_west.shape[0]
    corners = [edge_rows(from_north, from_south, count * halves + n) for n in range(2 * parts)]
    for i in range(count):
        wide[i, :tile_lat, :tile_lon] = fields[i]
        wide[i, :tile_lat, tile_lon:] = unpack_columns(from_west, from_east, i)
        for h in range(halves):
            wide[i, tile_lat:, h * BLOCK : (h + 1) * BLOCK] = edge_rows(from_north, from_south, i * halves + h)
        wide[i, tile_lat:, tile_lon:] = unpack_columns(corners[:parts], corners[parts:], i)


def place_sums(first, sums, from_north, from_south, payload):
    lon_count, parts, tile_lat = sums.shape[:3]
    for k in range(lon_count):
        for part in range(parts):
            payload[k, part, :tile_lat] = sums[k, part]
            payload[k, part, tile_lat:] = edge_rows(from_north, from_south, first + k * parts + part)


def eastward(x):
    return turn(x, -1, 1)


def westward(x):
    return turn(x, 1, 1)


def northward(x):
    return turn(x, -1, 0)


def southward(x):
    return turn(x, 1, 0)


def run_adjoint(
    fields, from_west, from_east, from_north, from_south, adjoint_out, blocks, coeffs, start, wide, state
):
    levels = adjoint_out.shape[1]
    tile_lat, tile_lon = fields.shape[1:]
    widen(fields, from_west, from_east, from_north, from_south, wide)
    base = 4 * levels
    for f in range(2):
        for level in range(levels):
            start[f, level] = wide[f * levels + level]
    mask0 = None
    for level in range(levels):
        east_d, east_u = wide[base + level], wide[base + levels + level]
        north_d, north_u = wide[base + 2 * levels + level], wide[base + 3 * levels + level]
        mask = (east_d > 0.0).astype(f32)
        mask0 = mask if mask0 is None else mask0
        mask_e, mask_n = eastward(mask), northward(mask)
        east_k, east_v = east_d * mask_e, east_u * mask_e
        north_k, north_v = north_d * mask_n, north_u * mask_n
        coeffs[0, level] = jnp.maximum(east_v, 0.0) + east_k
        coeffs[1, level] = jnp.minimum(east_v, 0.0) - east_k
        coeffs[2, level] = jnp.maximum(north_v, 0.0) + north_k
        coeffs[3, level] = jnp.minimum(north_v, 0.0) - north_k
        coeffs[4, level] = wide[base + 4 * levels + level] if level < levels - 1 else jnp.zeros_like(mask)
        coeffs[5, level] = mask
    for f in range(2):
        surface = jnp.zeros((tile_lat, tile_lon), f32)
        for step in range(STEPS):
            above = None
            for level in range(levels):
                source = wide.at[(2 + f) * levels + level] if step == 0 else state.at[(step - 1) % 2, level]
                lam = source[...]
                if level == 0:
                    surface = surface + lam[:tile_lat, :tile_lon]
                step_x = eastward(lam) - lam
                step_y = northward(lam) - lam
                out = lam + coeffs[0, level] * step_x + westward(coeffs[1, level] * step_x)
                out = out + coeffs[2, level] * step_y + southward(coeffs[3, level] * step_y)
                if level < levels - 1:
                    if step == 0:
                        lower = wide[(2 + f) * levels + level + 1]
                    else:
                        lower = state[(step - 1) % 2, level + 1]
                    vertical = coeffs[4, level] * (lower - lam)
                    out = out + vertical
                if above is not None:
                    out = out - above
                above = vertical if level < levels - 1 else None
                if step == STEPS - 1:
                    adjoint_out[f, level] = out[:tile_lat, :tile_lon]
                else:
                    state[step % 2, level] = out
        surface = surface * mask0[:tile_lat, :tile_lon]
        halves = tile_lon // BLOCK
        for h in range(halves):
            at = (f * halves + h) * tile_lat
            for k in range(blocks.shape[0]):
                blocks[k, at : at + tile_lat] = surface[:, h * BLOCK : (h + 1) * BLOCK]


def run_forward(coeffs, start, received, final, state):
    levels = coeffs.shape[1]
    tile_lat, tile_lon = final.shape[2:]
    halves = tile_lon // BLOCK
    total = [
        sum((received[j, part] for j in range(1, received.shape[0])), received[0, part])
        for part in range(received.shape[1])
    ]
    lane = lanes(total[0].shape)
    for f in range(2):
        edge = total[2 * halves]
        if f == 1:
            edge = jnp.where(lane < HALO, turn(edge, -HALO, 1), turn(edge, HALO, 1))
        edge = jnp.where((lane < HALO) | (lane >= BLOCK - HALO), edge, 0.0)
        force = jnp.concatenate([*total[f * halves : (f + 1) * halves], edge], axis=1)
        force = force * coeffs[5, 0]
        for step in range(STEPS):
            above = None
            for level in range(levels):
                read = (lambda n: start[f, n]) if step == 0 else (lambda n: state[(step - 1) % 2, n])
                theta = read(level)
                east_flux = coeffs[0, level] * theta + coeffs[1, level] * eastward(theta)
                north_flux = coeffs[2, level] * theta + coeffs[3, level] * northward(theta)
                out = theta - (east_flux - westward(east_flux)) - (north_flux - southward(north_flux))
                if level < levels - 1:
                    vertical = coeffs[4, level] * (theta - read(level + 1))
                    out = out - vertical
                if above is not None:
                    out = out + above
                above = vertical if level < levels - 1 else None
                if level == 0:
                    out = out + force
                if step == STEPS - 1:
                    final[f, level] = out[:tile_lat, :tile_lon]
                else:
                    state[step % 2, level] = out


def split(x):
    high = x.astype(bf16)
    return high, (x - high.astype(f32)).astype(bf16)


def as_column(ids):
    n = ids.shape[1]
    shape = (n, n)
    return jnp.sum(
        jnp.where(rows(shape) == lanes(shape), jnp.broadcast_to(ids.astype(f32), shape), 0.0),
        axis=1,
        keepdims=True,
    )


def one_hot(where):
    return jnp.where(where, 1.0, 0.0).astype(bf16)


def fetch_group(weights, first, held, arrived, g):
    return pltpu.make_async_copy(
        weights.at[pl.ds((first + g) * GROUP, GROUP)], held.at[g], arrived.at[g]
    )


def fetch_weights(weights, first, held, arrived):
    for g in range(held.shape[0]):
        fetch_group(weights, first, held, arrived, g).start()


def apply_weights(weights, first, held, arrived, vectors, picks, total, transposed):
    def group(g, carry):
        left, right = [[], []], []
        fetch_group(weights, first, held, arrived, g).wait()
        for u in range(GROUP):
            w = (first + g) * GROUP + u
            here = picks[...] == lax.convert_element_type(w.astype(f32), bf16)
            here = jnp.concatenate([here, here], axis=1)
            for f in range(2):
                own = vectors[:, f * 2 * BLOCK : (f + 1) * 2 * BLOCK]
                left[f].append(jnp.where(here, own, jnp.zeros_like(own)))
            high, low = split(held[g, u])
            if transposed:
                both = jnp.concatenate([high, low], axis=1)
                right.append(jnp.concatenate([both, both], axis=0))
            else:
                both = jnp.concatenate([high, low], axis=0)
                right.append(jnp.concatenate([both, both], axis=1))
        right = jnp.concatenate(right, axis=0 if transposed else 1)
        contract = (((1,), (0 if transposed else 1,)), ((), ()))
        for f in range(2):
            product = lax.dot_general(
                jnp.concatenate(left[f], axis=1), right, contract, preferred_element_type=f32
            )
            total[f] += product
        return carry

    lax.fori_loop(0, held.shape[0], group, 0)


def slot_columns(ids, out_dtype=f32):
    return jnp.concatenate([as_column(ids[k : k + 1, :]) for k in range(ids.shape[0])], axis=0)


def weigh(
    atm_state, margins, weights, after, sums, vectors, picks, total, held, arrived, atm_near, ids, near
):
    lon_count, cap = margins.shape[3:]
    slots = lon_count * cap
    atm = atm_state.shape[2]
    tile_lat = sums.shape[2]
    copies = fetch([(margins, ids), (atm_state, atm_near)], near)
    fetch_weights(weights, 0, held, arrived)
    for copy in copies:
        copy.wait()
    ocean, atm_ids, block_ids = (ids[n, 0, 0] for n in range(3))
    picks[...] = jnp.broadcast_to(slot_columns(block_ids), (slots, BLOCK)).astype(bf16)
    parts = [part for f in range(2) for part in split(atm_near[f, 0])]
    table = jnp.concatenate(parts, axis=1)
    pick = one_hot(slot_columns(atm_ids).astype(jnp.int32) == lanes((slots, atm)))
    vectors[...] = jnp.dot(pick, table, preferred_element_type=f32).astype(bf16)
    total[...] = jnp.zeros_like(total)
    apply_weights(weights, 0, held, arrived, vectors, picks, total, False)
    ocean_blocks = 2 * tile_lat
    order = rows((ocean_blocks, cap))
    order = (order % tile_lat) * 2 + order // tile_lat
    lane = lanes((tile_lat, BLOCK))
    products = []
    for k in range(lon_count):
        place = one_hot(jnp.broadcast_to(ocean[k : k + 1, :], (ocean_blocks, cap)) == order)
        parts = []
        for f in range(2):
            value = total[f, k * cap : (k + 1) * cap]
            parts += split(value[:, :BLOCK] + value[:, BLOCK:])
        product = jnp.dot(place, jnp.concatenate(parts, axis=1), preferred_element_type=f32)
        products.append(
            [product[:, 2 * f * BLOCK : (2 * f + 1) * BLOCK] + product[:, (2 * f + 1) * BLOCK : (2 * f + 2) * BLOCK]
             for f in range(2)]
        )
        for f in range(2):
            for h in range(2):
                sums[k, 2 * f + h] = products[k][f][h * tile_lat : (h + 1) * tile_lat]
    for k in range(lon_count):
        after, before = products[(k + 1) % lon_count], products[(k - 1) % lon_count]
        edge = jnp.zeros((tile_lat, BLOCK), f32)
        for f in range(2):
            at = f * HALO
            edge = jnp.where((lane >= at) & (lane < at + HALO), turn(after[f][:tile_lat], at, 1), edge)
            end = BLOCK - at
            edge = jnp.where((lane >= end - HALO) & (lane < end), turn(before[f][tile_lat:], -at, 1), edge)
        sums[k, 4] = edge


def unweigh(gathered, margins, weights, gradient, vectors, picks, total, held, arrived, ids, near):
    lon_count, cap = margins.shape[3:]
    slots = lon_count * cap
    atm = gradient.shape[2]
    ocean_blocks = gathered.shape[1] // 2
    tile_lat = ocean_blocks // 2
    copies = fetch([(margins, ids)], near)
    fetch_weights(weights, 0, held, arrived)
    for copy in copies:
        copy.wait()
    ocean, atm_ids, block_ids = (ids[n, 0, 0] for n in range(3))
    picks[...] = jnp.broadcast_to(slot_columns(block_ids), (slots, BLOCK)).astype(bf16)
    order = lanes((cap, ocean_blocks))
    order = (order % tile_lat) * 2 + order // tile_lat
    for k in range(lon_count):
        pick = one_hot(as_column(ocean[k : k + 1, :]).astype(jnp.int32) == order)
        parts = [
            part for f in range(2) for part in split(gathered[k, f * ocean_blocks : (f + 1) * ocean_blocks])
        ]
        vectors[k * cap : (k + 1) * cap] = jnp.dot(
            pick, jnp.concatenate(parts, axis=1), preferred_element_type=f32
        ).astype(bf16)
    total[...] = jnp.zeros_like(total)
    apply_weights(weights, 0, held, arrived, vectors, picks, total, True)
    place = jnp.concatenate(
        [
            one_hot(jnp.broadcast_to(atm_ids[k : k + 1, :], (atm, cap)) == rows((atm, cap)))
            for k in range(lon_count)
        ],
        axis=1,
    )
    parts = [part for f in range(2) for part in split(total[f, :, :BLOCK] + total[f, :, BLOCK:])]
    product = jnp.dot(place, jnp.concatenate(parts, axis=1), preferred_element_type=f32)
    for f in range(2):
        at = 2 * f * BLOCK
        gradient[f, 0] = product[:, at : at + BLOCK] + product[:, at + BLOCK : at + 2 * BLOCK]


def on_device(tracers, cotangent, land_mask, diffusion, velocity, weights, atm_state, margins):
    levels, tile_lat, tile_lon = land_mask.shape
    lon_count, lat_count = lax.axis_size("lon"), lax.axis_size("lat")
    slots = lon_count * margins.shape[4]
    halves = tile_lon // BLOCK
    count = 9 * levels - 1
    parts = -(-count // PER_LANES)
    to_next = [(i, (i + 1) % lon_count) for i in range(lon_count)]
    to_prev = [(j, i) for i, j in to_next]
    up = [(i, i + 1) for i in range(lat_count - 1)]
    down = [(j, i) for i, j in up]
    inputs = (tracers, cotangent, land_mask, diffusion, velocity)

    def in_vmem(s):
        return pltpu.VMEM(s.shape, s.dtype)

    message = (parts, tile_lat, BLOCK)
    fields, to_west, to_east = call(
        pack_columns,
        [(count, tile_lat, tile_lon), message, message],
        [*map(in_vmem, inputs), pltpu.SemaphoreType.DMA((5,))],
        name="pack_columns",
        inputs=5,
        far=range(5),
    )(*inputs)
    from_east = lax.ppermute(to_west, "lon", to_prev)
    from_west = lax.ppermute(to_east, "lon", to_next)

    groups = weights.shape[0] // GROUP
    coupling_scratch = [
        pltpu.VMEM((slots, 4 * BLOCK), bf16),
        pltpu.VMEM((slots, BLOCK), bf16),
        pltpu.VMEM((2, slots, 2 * BLOCK), f32),
        pltpu.VMEM((groups, GROUP, BLOCK, BLOCK), f32),
        pltpu.SemaphoreType.DMA((groups,)),
    ]
    coupling_flops = 4 * slots * weights.shape[0] * 4 * BLOCK * BLOCK * 2
    sum_parts = 2 * halves + 1
    (sums,) = call(
        weigh,
        [(lon_count, sum_parts, tile_lat, BLOCK)],
        [*coupling_scratch, in_vmem(atm_state), in_vmem(margins), pltpu.SemaphoreType.DMA((2,))],
        coupling_flops,
        name="weigh",
        inputs=4,
        far=range(3),
    )(atm_state, margins, weights, to_west)

    sources = count * halves + 2 * parts + lon_count * sum_parts
    message = (-(-sources // 2), 8, BLOCK)
    to_north, to_south = call(pack_rows, [message, message], name="pack_rows", inputs=4)(
        fields, from_west, from_east, sums
    )
    from_south = lax.ppermute(to_north, "lat", up)
    from_north = lax.ppermute(to_south, "lat", down)

    (payload,) = call(
        functools.partial(place_sums, sources - lon_count * sum_parts),
        [(lon_count, sum_parts, tile_lat + 8, BLOCK)],
        name="place_sums",
        inputs=3,
    )(sums, from_north, from_south)
    received = lax.all_to_all(payload, "lon", split_axis=0, concat_axis=0, tiled=True)

    wide = (tile_lat + 8, tile_lon + BLOCK)
    adjoint, blocks, coeffs, start = call(
        run_adjoint,
        [
            cotangent.shape,
            (lon_count, 2 * halves * tile_lat, BLOCK),
            (6, levels, *wide),
            (2, levels, *wide),
        ],
        [pltpu.VMEM((count, *wide), f32), pltpu.VMEM((2, levels, *wide), f32)],
        name="run_adjoint",
        inputs=5,
    )(fields, from_west, from_east, from_north, from_south)
    gathered = lax.all_to_all(blocks, "lon", split_axis=0, concat_axis=0, tiled=True)

    (final,) = call(
        run_forward,
        [tracers.shape],
        [pltpu.VMEM((2, levels, *wide), f32)],
        name="run_forward",
        inputs=3,
    )(coeffs, start, received)

    (gradient,) = call(
        unweigh,
        [atm_state.shape],
        [*coupling_scratch, in_vmem(margins), pltpu.SemaphoreType.DMA((1,))],
        coupling_flops,
        name="unweigh",
        inputs=3,
        far=(1, 2),
    )(gathered, margins, weights)
    return (final, adjoint, gradient)


def solution(mesh):
    return jax.shard_map(
        on_device,
        mesh=mesh,
        in_specs=(
            P(None, None, "lat", "lon"),
            P(None, None, "lat", "lon"),
            P(None, "lat", "lon"),
            P(None, None, "lat", "lon"),
            P(None, None, "lat", "lon"),
            P(),
            P(None, "lat", "lon", None),
            P(None, "lat", "lon", None, None),
        ),
        out_specs=(
            P(None, None, "lat", "lon"),
            P(None, None, "lat", "lon"),
            P(None, "lat", "lon", None),
        ),
        check_vma=False,
    )
```

profile of v0, /device:TPU:0, one launch (start us, length us, event | category | flops | bytes accessed | tf_op | source)
XLA Modules:
  0.0 60.3 jit_solution(1869535946784972237)
XLA Ops:
  0.6 1.4 %pack_columns.1 = (f32[35,16,256]{2,1,0:T(8,128)S(1)}, f32[2,16,128]{2,1,0:T(8,128)S(1)}, f32[2,16,128]{2,1,0:T(8,128)S(1)}) custom-call(f32[2,4,16,256]{3,2,1,0:T(8,128)} %refs_0_.1, f32[2,4,16,256]{3,2,1,0:T(8,128)} %refs_1_.1, s32[4,16,256]{2,1,0:T(8,128)} %refs_2_.1, f32[3,4,16,256]{3,2,1,0:T(8,128)} %refs_3_.1, f32[2,4,16,256]{3,2,1,0:T(8,128)} %refs_4_.1), custom_call_target="tpu_custom_call" | custom-call | bytes 1048576 | tf_op jit(solution)/shard_map/pack_columns/pallas_call | solution.py:35
  2.1 6.0 %collective-permute-start.1 = (f32[2,16,128]{2,1,0:T(8,128)S(1)}, f32[2,16,128]{2,1,0:T(8,128)S(1)}, u32[]{:S(2)}, u32[]{:S(2)}) collective-permute-start(f32[2,16,128]{2,1,0:T(8,128)S(1)} %get-tuple-element.14.after), channel_id=1, source_target_pairs={{1,0},{2,1},{3,2},{4,3},{5,4},{6,5},{7,6},{0,7},{9,8},{10,9},{11,1... | collective-permute-start | bytes 49160 | tf_op jit(solution)/shard_map/ppermute | solution.py:443
  8.1 0.0 collective-permute-start
  8.1 8.6 %weigh.1.sums = f32[8,5,16,128]{3,2,1,0:T(8,128)S(1)} custom-call(f32[2,1,256,128]{3,2,1,0:T(8,128)} %atm_state.1, s32[3,1,1,8,64]{4,3,2,1,0:T(8,128)} %margins.3, f32[32,128,128]{2,1,0:T(8,128)} %weights.3, f32[2,16,128]{2,1,0:T(8,128)S(1)} %get-tuple-element.14.after), custom_call_target="tpu_custom_call" | custom-call | flops 8589934592 | bytes 1048576 | tf_op jit(solution)/shard_map/weigh/pallas_call | solution.py:35
  16.7 0.0 collective-permute-done.1.from_east
  16.7 0.0 collective-permute-done.from_west
  16.7 0.1 pack_rows.1
  16.8 1.3 %collective-permute-start.2 = (f32[57,8,128]{2,1,0:T(8,128)S(1)}, f32[57,8,128]{2,1,0:T(8,128)S(1)}, u32[]{:S(2)}, u32[]{:S(2)}) collective-permute-start(f32[57,8,128]{2,1,0:T(8,128)S(1)} %get-tuple-element.15), channel_id=1, source_target_pairs={{8,0},{16,8},{24,16},{9,1},{17,9},{25,17},{10,2},{18,10},{26,18},{... | collective-permute-start | bytes 700424 | tf_op jit(solution)/shard_map/ppermute | solution.py:472
  18.1 3.0 %collective-permute-start.3 = (f32[57,8,128]{2,1,0:T(8,128)S(1)}, f32[57,8,128]{2,1,0:T(8,128)S(1)}, u32[]{:S(2)}, u32[]{:S(2)}) collective-permute-start(f32[57,8,128]{2,1,0:T(8,128)S(1)} %get-tuple-element.16), channel_id=1, source_target_pairs={{0,8},{8,16},{16,24},{1,9},{9,17},{17,25},{2,10},{10,18},{18,26},{... | collective-permute-start | bytes 700424 | tf_op jit(solution)/shard_map/ppermute | solution.py:471
  21.1 0.0 collective-permute-done.2.from_north
  21.1 1.1 %collective-permute-done.3.from_south = f32[57,8,128]{2,1,0:T(8,128)S(1)} collective-permute-done((f32[57,8,128]{2,1,0:T(8,128)S(1)}, f32[57,8,128]{2,1,0:T(8,128)S(1)}, u32[]{:S(2)}, u32[]{:S(2)}) %collective-permute-start.3) | collective-permute-done | bytes 233504 | tf_op jit(solution)/shard_map/ppermute | solution.py:471
  22.2 2.5 %run_adjoint.1 = (f32[2,4,16,256]{3,2,1,0:T(8,128)}, f32[8,64,128]{2,1,0:T(8,128)}, f32[6,4,24,384]{3,2,1,0:T(8,128)S(1)}, f32[2,4,24,384]{3,2,1,0:T(8,128)S(1)}) custom-call(f32[35,16,256]{2,1,0:T(8,128)S(1)} %get-tuple-element.12.fields, f32[2,16,128]{2,1,0:T(8,128)S(1)} %collective-permute-done.from_west, ...), custom_call_target="tpu_custom_call" | custom-call | bytes 1048576 | tf_op jit(solution)/shard_map/run_adjoint/pallas_call | solution.py:35
  24.7 6.0 %all-to-all-start.1 = ((f32[8,64,128]{2,1,0:T(8,128)}), f32[8,64,128]{2,1,0:T(8,128)S(1)}, u32[]{:S(2)}, u32[]{:S(2)}) async-start(f32[8,64,128]{2,1,0:T(8,128)} %get-tuple-element.20), calls=%async_computation.1 | async-start | bytes 524288 | tf_op jit(solution)/shard_map/all_to_all | solution.py:495
  30.7 0.8 %place_sums.1 = f32[8,5,24,128]{3,2,1,0:T(8,128)} custom-call(f32[8,5,16,128]{3,2,1,0:T(8,128)S(1)} %weigh.1.sums, f32[57,8,128]{2,1,0:T(8,128)S(1)} %collective-permute-done.2.from_north, f32[57,8,128]{2,1,0:T(8,128)S(1)} %collective-permute-done.3.from_south), custom_call_target="tpu_custom_call" | custom-call | bytes 1048576 | tf_op jit(solution)/shard_map/place_sums/pallas_call | solution.py:35
  31.6 7.5 %all-to-all-done.1.gathered = f32[8,64,128]{2,1,0:T(8,128)S(1)} async-done(((f32[8,64,128]{2,1,0:T(8,128)}), f32[8,64,128]{2,1,0:T(8,128)S(1)}, u32[]{:S(2)}, u32[]{:S(2)}) %all-to-all-start.1) | async-done | bytes 262176 | tf_op jit(solution)/shard_map/all_to_all | solution.py:495
  39.1 4.8 %all-to-all-start = ((f32[8,5,24,128]{3,2,1,0:T(8,128)}), f32[8,5,24,128]{3,2,1,0:T(8,128)S(1)}, u32[]{:S(2)}, u32[]{:S(2)}) async-start(f32[8,5,24,128]{3,2,1,0:T(8,128)} %place_sums.1), calls=%async_computation | async-start | bytes 983040 | tf_op jit(solution)/shard_map/all_to_all | solution.py:480
  43.9 8.5 %unweigh.1 = f32[2,1,256,128]{3,2,1,0:T(8,128)} custom-call(f32[8,64,128]{2,1,0:T(8,128)S(1)} %all-to-all-done.1.gathered, s32[3,1,1,8,64]{4,3,2,1,0:T(8,128)} %margins.3, f32[32,128,128]{2,1,0:T(8,128)} %weights.3), custom_call_target="tpu_custom_call" | custom-call | flops 8589934592 | bytes 1048576 | tf_op jit(solution)/shard_map/unweigh/pallas_call | solution.py:35
  52.4 6.1 %all-to-all-done.received = f32[8,5,24,128]{3,2,1,0:T(8,128)S(1)} async-done(((f32[8,5,24,128]{3,2,1,0:T(8,128)}), f32[8,5,24,128]{3,2,1,0:T(8,128)S(1)}, u32[]{:S(2)}, u32[]{:S(2)}) %all-to-all-start) | async-done | bytes 491552 | tf_op jit(solution)/shard_map/all_to_all | solution.py:480
  58.6 1.7 %run_forward.1 = f32[2,4,16,256]{3,2,1,0:T(8,128)} custom-call(f32[6,4,24,384]{3,2,1,0:T(8,128)S(1)} %get-tuple-element.17.coeffs, f32[2,4,24,384]{3,2,1,0:T(8,128)S(1)} %get-tuple-element.18.start, f32[8,5,24,128]{3,2,1,0:T(8,128)S(1)} %all-to-all-done.received), custom_call_target="tpu_custom_call" | custom-call | bytes 1048576 | tf_op jit(solution)/shard_map/run_forward/pallas_call | solution.py:35
Async XLA Ops:
  2.1 14.6 %collective-permute-start.1 = (f32[2,16,128]{2,1,0:T(8,128)S(1)}, f32[2,16,128]{2,1,0:T(8,128)S(1)}, u32[]{:S(2)}, u32[]{:S(2)}) collective-permute-start(f32[2,16,128]{2,1,0:T(8,128)S(1)} %get-tuple-element.14.after), channel_id=1, source_target_pairs={{1,0},{2,1},{3,2},{4,3},{5,4},{6,5},{7,6},{0,7},{9,8},{10,9},{11,1... | collective-permute-start | bytes 49160 | tf_op jit(solution)/shard_map/ppermute | solution.py:443
  8.1 8.6 %collective-permute-start = (f32[2,16,128]{2,1,0:T(8,128)S(1)}, f32[2,16,128]{2,1,0:T(8,128)S(1)}, u32[]{:S(2)}, u32[]{:S(2)}) collective-permute-start(f32[2,16,128]{2,1,0:T(8,128)S(1)} %get-tuple-element.13), channel_id=1, source_target_pairs={{0,1},{1,2},{2,3},{3,4},{4,5},{5,6},{6,7},{7,0},{8,9},{9,10},{10,1... | collective-permute-start | bytes 49160 | tf_op jit(solution)/shard_map/ppermute | solution.py:444
  16.8 4.4 %collective-permute-start.2 = (f32[57,8,128]{2,1,0:T(8,128)S(1)}, f32[57,8,128]{2,1,0:T(8,128)S(1)}, u32[]{:S(2)}, u32[]{:S(2)}) collective-permute-start(f32[57,8,128]{2,1,0:T(8,128)S(1)} %get-tuple-element.15), channel_id=1, source_target_pairs={{8,0},{16,8},{24,16},{9,1},{17,9},{25,17},{10,2},{18,10},{26,18},{... | collective-permute-start | bytes 700424 | tf_op jit(solution)/shard_map/ppermute | solution.py:472
  18.1 4.1 %collective-permute-start.3 = (f32[57,8,128]{2,1,0:T(8,128)S(1)}, f32[57,8,128]{2,1,0:T(8,128)S(1)}, u32[]{:S(2)}, u32[]{:S(2)}) collective-permute-start(f32[57,8,128]{2,1,0:T(8,128)S(1)} %get-tuple-element.16), channel_id=1, source_target_pairs={{0,8},{8,16},{16,24},{1,9},{9,17},{17,25},{2,10},{10,18},{18,26},{... | collective-permute-start | bytes 700424 | tf_op jit(solution)/shard_map/ppermute | solution.py:471
  24.7 14.3 %all-to-all-start.1 = ((f32[8,64,128]{2,1,0:T(8,128)}), f32[8,64,128]{2,1,0:T(8,128)S(1)}, u32[]{:S(2)}, u32[]{:S(2)}) async-start(f32[8,64,128]{2,1,0:T(8,128)} %get-tuple-element.20), calls=%async_computation.1 | async-start | bytes 524288 | tf_op jit(solution)/shard_map/all_to_all | solution.py:495
  39.1 19.5 %all-to-all-start = ((f32[8,5,24,128]{3,2,1,0:T(8,128)}), f32[8,5,24,128]{3,2,1,0:T(8,128)S(1)}, u32[]{:S(2)}, u32[]{:S(2)}) async-start(f32[8,5,24,128]{3,2,1,0:T(8,128)} %place_sums.1), calls=%async_computation | async-start | bytes 983040 | tf_op jit(solution)/shard_map/all_to_all | solution.py:480
where the time goes:
time: 60.7 us; the launch traced here: 60.3 us
  Pallas kernels  23.7 us (39%)
  starting transfers between devices  21.2 us (35%)
  waiting for transfers between devices  14.7 us (24%)
  between operations  0.7 us (1%)
    pallas_call x7, Pallas kernels, run(): kernel(*(pltpu.with_memory_space_constraint(x, pltpu.HBM) if n in far els...  23.7 us
    all_to_all x1, waiting for transfers between devices, on_device(): lax.all_to_all(blocks, 'lon', split_axis=0, concat_axis=0, tiled=True)  7.48 us
    all_to_all x1, waiting for transfers between devices, on_device(): lax.all_to_all(payload, 'lon', split_axis=0, concat_axis=0, tiled=True)  6.12 us
    ppermute x1, starting transfers between devices, on_device(): from_east = lax.ppermute(to_west, 'lon', to_prev)  6.03 us
    all_to_all x1, starting transfers between devices, on_device(): lax.all_to_all(blocks, 'lon', split_axis=0, concat_axis=0, tiled=True)  6.01 us
    all_to_all x1, starting transfers between devices, on_device(): lax.all_to_all(payload, 'lon', split_axis=0, concat_axis=0, tiled=True)  4.82 us
    ppermute x1, starting transfers between devices, on_device(): from_south = lax.ppermute(to_north, 'lat', up)  3.04 us
    ppermute x1, starting transfers between devices, on_device(): from_north = lax.ppermute(to_south, 'lat', down)  1.29 us
  transfers between devices with their start and end apart: 6, of which 3 were waited for; matrix products, arithmetic and copies ran while one was open for 0% of the time, Pallas kernels for 30%

commit v1 on v0

--- a/solution.py
+++ b/solution.py
@@ -1,5 +1,3 @@
-import functools
-
 import jax
 import jax.numpy as jnp
 from jax import lax
@@ -101,16 +99,16 @@
     return jnp.where(lane < HALO, east, jnp.where(lane >= BLOCK - HALO, west, 0.0))
 
 
-def row_sources(fields, from_west, from_east, sums):
+def row_sources(fields, from_west, from_east):
     out = [(fields, (i, slice(None), slice(h * BLOCK, (h + 1) * BLOCK)))
            for i in range(fields.shape[0]) for h in range(fields.shape[2] // BLOCK)]
     for columns in (from_west, from_east):
         out += [(columns, (part,)) for part in range(columns.shape[0])]
-    return out + [(sums, (k, part)) for k in range(sums.shape[0]) for part in range(sums.shape[1])]
-
-
-def pack_rows(fields, from_west, from_east, sums, to_north, to_south):
-    sources = [ref[at] for ref, at in row_sources(fields, from_west, from_east, sums)]
+    return out
+
+
+def pack_rows(fields, from_west, from_east, to_north, to_south):
+    sources = [ref[at] for ref, at in row_sources(fields, from_west, from_east)]
     half = to_north.shape[0]
     row = rows((8, BLOCK))
     for i in range(half):
@@ -140,14 +138,6 @@
         for h in range(halves):
             wide[i, tile_lat:, h * BLOCK : (h + 1) * BLOCK] = edge_rows(from_north, from_south, i * halves + h)
         wide[i, tile_lat:, tile_lon:] = unpack_columns(corners[:parts], corners[parts:], i)
-
-
-def place_sums(first, sums, from_north, from_south, payload):
-    lon_count, parts, tile_lat = sums.shape[:3]
-    for k in range(lon_count):
-        for part in range(parts):
-            payload[k, part, :tile_lat] = sums[k, part]
-            payload[k, part, tile_lat:] = edge_rows(from_north, from_south, first + k * parts + part)
 
 
 def eastward(x):
@@ -226,21 +216,40 @@
                 blocks[k, at : at + tile_lat] = surface[:, h * BLOCK : (h + 1) * BLOCK]
 
 
-def run_forward(coeffs, start, received, final, state):
-    levels = coeffs.shape[1]
-    tile_lat, tile_lon = final.shape[2:]
-    halves = tile_lon // BLOCK
+def sum_forcing(received, forcing, to_north, to_south):
+    tile_lat = forcing.shape[1]
+    halves = forcing.shape[2] // BLOCK - 1
     total = [
         sum((received[j, part] for j in range(1, received.shape[0])), received[0, part])
         for part in range(received.shape[1])
     ]
-    lane = lanes(total[0].shape)
+    lane = lanes((tile_lat, BLOCK))
+    packed = total[2 * halves]
     for f in range(2):
-        edge = total[2 * halves]
-        if f == 1:
-            edge = jnp.where(lane < HALO, turn(edge, -HALO, 1), turn(edge, HALO, 1))
-        edge = jnp.where((lane < HALO) | (lane >= BLOCK - HALO), edge, 0.0)
-        force = jnp.concatenate([*total[f * halves : (f + 1) * halves], edge], axis=1)
+        for h in range(halves):
+            forcing[f, :, h * BLOCK : (h + 1) * BLOCK] = total[f * halves + h]
+        near = (lane < HALO) | (lane >= BLOCK - HALO)
+        if f == 0:
+            edge = packed
+        else:
+            edge = jnp.where(lane < HALO, turn(packed, -HALO, 1), turn(packed, HALO, 1))
+        forcing[f, :, halves * BLOCK :] = jnp.where(near, edge, 0.0)
+    row = rows((8, forcing.shape[2]))
+    to_north[...] = jnp.where(row < HALO, turn(forcing[0, tile_lat - 8 :], HALO, 0), forcing[1, tile_lat - 8 :])
+    to_south[...] = jnp.where(row < HALO, forcing[0, :8], turn(forcing[1, :8], HALO, 0))
+
+
+def run_forward(coeffs, start, forcing, from_north, from_south, final, state):
+    levels = coeffs.shape[1]
+    tile_lat, tile_lon = final.shape[2:]
+    row = rows((8, forcing.shape[2]))
+    mask = None
+    for f in range(2):
+        if f == 0:
+            north, south = from_north[...], turn(from_south[...], HALO, 0)
+        else:
+            north, south = turn(from_north[...], HALO, 0), from_south[...]
+        force = jnp.concatenate([forcing[f], jnp.where(row < HALO, north, south)], axis=0)
         force = force * coeffs[5, 0]
         for step in range(STEPS):
             above = None
@@ -269,150 +278,186 @@
     return high, (x - high.astype(f32)).astype(bf16)
 
 
-def as_column(ids):
-    n = ids.shape[1]
-    shape = (n, n)
-    return jnp.sum(
-        jnp.where(rows(shape) == lanes(shape), jnp.broadcast_to(ids.astype(f32), shape), 0.0),
-        axis=1,
-        keepdims=True,
-    )
+def weight_copies(weights, held, arrived):
+    for g in range(held.shape[0]):
+        yield pltpu.make_async_copy(weights.at[pl.ds(g * GROUP, GROUP)], held.at[g], arrived.at[g])
+
+
+def fetch_weights(weights, held, arrived):
+    for copy in weight_copies(weights, held, arrived):
+        copy.start()
+
+
+def wait_weights(weights, held, arrived):
+    for copy in weight_copies(weights, held, arrived):
+        copy.wait()
 
 
 def one_hot(where):
     return jnp.where(where, 1.0, 0.0).astype(bf16)
 
 
-def fetch_group(weights, first, held, arrived, g):
-    return pltpu.make_async_copy(
-        weights.at[pl.ds((first + g) * GROUP, GROUP)], held.at[g], arrived.at[g]
-    )
-
-
-def fetch_weights(weights, first, held, arrived):
-    for g in range(held.shape[0]):
-        fetch_group(weights, first, held, arrived, g).start()
-
-
-def apply_weights(weights, first, held, arrived, vectors, picks, total, transposed):
-    def group(g, carry):
-        left, right = [[], []], []
-        fetch_group(weights, first, held, arrived, g).wait()
-        for u in range(GROUP):
-            w = (first + g) * GROUP + u
-            here = picks[...] == lax.convert_element_type(w.astype(f32), bf16)
-            here = jnp.concatenate([here, here], axis=1)
-            for f in range(2):
-                own = vectors[:, f * 2 * BLOCK : (f + 1) * 2 * BLOCK]
-                left[f].append(jnp.where(here, own, jnp.zeros_like(own)))
-            high, low = split(held[g, u])
-            if transposed:
-                both = jnp.concatenate([high, low], axis=1)
-                right.append(jnp.concatenate([both, both], axis=0))
-            else:
-                both = jnp.concatenate([high, low], axis=0)
-                right.append(jnp.concatenate([both, both], axis=1))
-        right = jnp.concatenate(right, axis=0 if transposed else 1)
-        contract = (((1,), (0 if transposed else 1,)), ((), ()))
-        for f in range(2):
-            product = lax.dot_general(
-                jnp.concatenate(left[f], axis=1), right, contract, preferred_element_type=f32
-            )
-            total[f] += product
+def places(slots, blocks):
+    return 8 * (-(-2 * slots // (8 * blocks)) + 1)
+
+
+def as_row(ids):
+    return jnp.concatenate([ids[k : k + 1, :] for k in range(ids.shape[0])], axis=1)
+
+
+def rank_slots(block_row, blocks):
+    slots = block_row.shape[1]
+    mine = rows((blocks, slots)) == block_row
+    upper = one_hot(rows((slots, slots)) < lanes((slots, slots)))
+    before = jnp.dot(one_hot(mine), upper, preferred_element_type=f32)
+    return jnp.sum(jnp.where(mine, before, 0.0), axis=0, keepdims=True)
+
+
+def couple(weights_near, ready, table, keys, block_row, rank, gather_first, transposed, result, scratch):
+    code, size = keys
+    column, vectors, products = scratch
+    slots = block_row.shape[1]
+    blocks = weights_near.shape[0] * weights_near.shape[1]
+    capacity = places(slots, blocks)
+    total_rows = column.shape[0]
+    result[...] = jnp.zeros_like(result)
+    rounds = jnp.max(rank).astype(jnp.int32) // capacity + 1
+
+    def one_round(r, carry):
+        place = rank.astype(jnp.int32) - r * capacity
+        place = jnp.where((place >= 0) & (place < capacity), block_row * capacity + place, -1)
+        eye = rows((BLOCK, BLOCK)) == lanes((BLOCK, BLOCK))
+        place_hot = []
+        for at in range(0, total_rows, BLOCK):
+            here = rows((BLOCK, slots)) + at == place
+            found = jnp.sum(jnp.where(here, code + 1.0, 0.0), axis=1, keepdims=True) - 1.0
+            found = jnp.broadcast_to(found, (BLOCK, BLOCK))
+            first = jnp.floor((found + 0.5) * (1.0 / size))
+            second = found - first * size
+            gather, put = (first, second) if gather_first else (second, first)
+            width = table.shape[0]
+            gather = jnp.concatenate([gather] * (width // BLOCK), axis=1)
+            hot = one_hot(gather == lanes((BLOCK, width)).astype(f32))
+            vectors[at : at + BLOCK] = jnp.dot(hot, table, preferred_element_type=f32)
+            put = jnp.sum(jnp.where(eye, put, 0.0), axis=0, keepdims=True)
+            place_hot.append(one_hot(rows((result.shape[0], BLOCK)).astype(f32) == put))
+        pl.when(r == 0)(ready)
+
+        def group(g, carry):
+            for u in range(GROUP):
+                at = pl.multiple_of((g * GROUP + u) * capacity, 8)
+                own = vectors[pl.ds(at, capacity)]
+                left = jnp.concatenate([own[:, n * BLOCK : (n + 1) * BLOCK] for n in range(4)], axis=0)
+                high, low = split(weights_near[g, u])
+                right = jnp.concatenate([high, low], axis=1 if transposed else 0)
+                contract = (((1,), (0 if transposed else 1,)), ((), ()))
+                product = lax.dot_general(left.astype(bf16), right, contract, preferred_element_type=f32)
+                for f in range(2):
+                    high_part = product[f * capacity : (f + 1) * capacity]
+                    low_part = product[(f + 2) * capacity : (f + 3) * capacity, :BLOCK]
+                    products[pl.ds(at, capacity), f * BLOCK : (f + 1) * BLOCK] = (
+                        high_part[:, BLOCK:] + low_part
+                    ) + high_part[:, :BLOCK]
+            return carry
+
+        lax.fori_loop(0, weights_near.shape[0], group, 0)
+        summed = jnp.dot(
+            jnp.concatenate(place_hot, axis=1),
+            jnp.concatenate(split(products[...]), axis=1),
+            preferred_element_type=f32,
+        )
+        result[...] += summed[:, : 2 * BLOCK] + summed[:, 2 * BLOCK :]
         return carry
 
-    lax.fori_loop(0, held.shape[0], group, 0)
-
-
-def slot_columns(ids, out_dtype=f32):
-    return jnp.concatenate([as_column(ids[k : k + 1, :]) for k in range(ids.shape[0])], axis=0)
-
-
-def weigh(
-    atm_state, margins, weights, after, sums, vectors, picks, total, held, arrived, atm_near, ids, near
-):
-    lon_count, cap = margins.shape[3:]
-    slots = lon_count * cap
+    lax.fori_loop(0, rounds, one_round, 0)
+
+
+def slot_keys(ids, tile_lat, atm):
+    lon_count, cap = ids.shape[3:]
+    ocean, atm_ids, block_ids = (ids[n, 0, 0] for n in range(3))
+    order = (ocean & 1) * tile_lat + (ocean >> 1) + rows((lon_count, cap)) * (2 * tile_lat)
+    order = jnp.where(ocean >= 0, order, lon_count * 2 * tile_lat)
+    return as_row((order * atm + atm_ids).astype(f32)), as_row(block_ids)
+
+
+def weigh(atm_state, margins, weights, after, sums, rank_out, result, *scratch):
+    scratch, (held, arrived, atm_near, ids, near) = scratch[:3], scratch[3:]
+    lon_count = margins.shape[3]
     atm = atm_state.shape[2]
     tile_lat = sums.shape[2]
     copies = fetch([(margins, ids), (atm_state, atm_near)], near)
-    fetch_weights(weights, 0, held, arrived)
+    fetch_weights(weights, held, arrived)
     for copy in copies:
         copy.wait()
-    ocean, atm_ids, block_ids = (ids[n, 0, 0] for n in range(3))
-    picks[...] = jnp.broadcast_to(slot_columns(block_ids), (slots, BLOCK)).astype(bf16)
-    parts = [part for f in range(2) for part in split(atm_near[f, 0])]
-    table = jnp.concatenate(parts, axis=1)
-    pick = one_hot(slot_columns(atm_ids).astype(jnp.int32) == lanes((slots, atm)))
-    vectors[...] = jnp.dot(pick, table, preferred_element_type=f32).astype(bf16)
-    total[...] = jnp.zeros_like(total)
-    apply_weights(weights, 0, held, arrived, vectors, picks, total, False)
-    ocean_blocks = 2 * tile_lat
-    order = rows((ocean_blocks, cap))
-    order = (order % tile_lat) * 2 + order // tile_lat
+    code, block_row = slot_keys(ids, tile_lat, atm)
+    rank = rank_slots(block_row, weights.shape[0])
+    rank_out[...] = rank
+    parts = [split(atm_near[f, 0]) for f in range(2)]
+    table = jnp.concatenate([parts[f][n] for n in range(2) for f in range(2)], axis=1)
+    couple(
+        held,
+        lambda: wait_weights(weights, held, arrived),
+        table,
+        (code, atm),
+        block_row,
+        rank,
+        False,
+        False,
+        result,
+        scratch,
+    )
     lane = lanes((tile_lat, BLOCK))
-    products = []
+
+    def block_sums(k, f, h):
+        at = (2 * k + h) * tile_lat
+        return result[at : at + tile_lat, f * BLOCK : (f + 1) * BLOCK]
+
     for k in range(lon_count):
-        place = one_hot(jnp.broadcast_to(ocean[k : k + 1, :], (ocean_blocks, cap)) == order)
-        parts = []
-        for f in range(2):
-            value = total[f, k * cap : (k + 1) * cap]
-            parts += split(value[:, :BLOCK] + value[:, BLOCK:])
-        product = jnp.dot(place, jnp.concatenate(parts, axis=1), preferred_element_type=f32)
-        products.append(
-            [product[:, 2 * f * BLOCK : (2 * f + 1) * BLOCK] + product[:, (2 * f + 1) * BLOCK : (2 * f + 2) * BLOCK]
-             for f in range(2)]
-        )
+        edge = jnp.zeros((tile_lat, BLOCK), f32)
         for f in range(2):
             for h in range(2):
-                sums[k, 2 * f + h] = products[k][f][h * tile_lat : (h + 1) * tile_lat]
-    for k in range(lon_count):
-        after, before = products[(k + 1) % lon_count], products[(k - 1) % lon_count]
-        edge = jnp.zeros((tile_lat, BLOCK), f32)
-        for f in range(2):
+                sums[k, 2 * f + h] = block_sums(k, f, h)
             at = f * HALO
-            edge = jnp.where((lane >= at) & (lane < at + HALO), turn(after[f][:tile_lat], at, 1), edge)
+            after = turn(block_sums((k + 1) % lon_count, f, 0), at, 1)
+            before = turn(block_sums((k - 1) % lon_count, f, 1), -at, 1)
+            edge = jnp.where((lane >= at) & (lane < at + HALO), after, edge)
             end = BLOCK - at
-            edge = jnp.where((lane >= end - HALO) & (lane < end), turn(before[f][tile_lat:], -at, 1), edge)
+            edge = jnp.where((lane >= end - HALO) & (lane < end), before, edge)
         sums[k, 4] = edge
 
 
-def unweigh(gathered, margins, weights, gradient, vectors, picks, total, held, arrived, ids, near):
-    lon_count, cap = margins.shape[3:]
-    slots = lon_count * cap
+def unweigh(gathered, rank, margins, weights, gradient, result, *scratch):
+    scratch, (held, arrived, ids, near) = scratch[:3], scratch[3:]
     atm = gradient.shape[2]
-    ocean_blocks = gathered.shape[1] // 2
-    tile_lat = ocean_blocks // 2
+    lon_count, ocean_blocks = gathered.shape[0], gathered.shape[1] // 2
     copies = fetch([(margins, ids)], near)
-    fetch_weights(weights, 0, held, arrived)
+    fetch_weights(weights, held, arrived)
     for copy in copies:
         copy.wait()
-    ocean, atm_ids, block_ids = (ids[n, 0, 0] for n in range(3))
-    picks[...] = jnp.broadcast_to(slot_columns(block_ids), (slots, BLOCK)).astype(bf16)
-    order = lanes((cap, ocean_blocks))
-    order = (order % tile_lat) * 2 + order // tile_lat
-    for k in range(lon_count):
-        pick = one_hot(as_column(ocean[k : k + 1, :]).astype(jnp.int32) == order)
-        parts = [
-            part for f in range(2) for part in split(gathered[k, f * ocean_blocks : (f + 1) * ocean_blocks])
-        ]
-        vectors[k * cap : (k + 1) * cap] = jnp.dot(
-            pick, jnp.concatenate(parts, axis=1), preferred_element_type=f32
-        ).astype(bf16)
-    total[...] = jnp.zeros_like(total)
-    apply_weights(weights, 0, held, arrived, vectors, picks, total, True)
-    place = jnp.concatenate(
-        [
-            one_hot(jnp.broadcast_to(atm_ids[k : k + 1, :], (atm, cap)) == rows((atm, cap)))
-            for k in range(lon_count)
-        ],
-        axis=1,
+    code, block_row = slot_keys(ids, ocean_blocks // 2, atm)
+    parts = [
+        split(
+            jnp.concatenate(
+                [gathered[k, f * ocean_blocks : (f + 1) * ocean_blocks] for k in range(lon_count)], axis=0
+            )
+        )
+        for f in range(2)
+    ]
+    table = jnp.concatenate([parts[f][n] for n in range(2) for f in range(2)], axis=1)
+    couple(
+        held,
+        lambda: wait_weights(weights, held, arrived),
+        table,
+        (code, atm),
+        block_row,
+        rank[...],
+        True,
+        True,
+        result,
+        scratch,
     )
-    parts = [part for f in range(2) for part in split(total[f, :, :BLOCK] + total[f, :, BLOCK:])]
-    product = jnp.dot(place, jnp.concatenate(parts, axis=1), preferred_element_type=f32)
     for f in range(2):
-        at = 2 * f * BLOCK
-        gradient[f, 0] = product[:, at : at + BLOCK] + product[:, at + BLOCK : at + 2 * BLOCK]
+        gradient[f, 0] = result[:, f * BLOCK : (f + 1) * BLOCK]
 
 
 def on_device(tracers, cotangent, land_mask, diffusion, velocity, weights, atm_state, margins):
@@ -443,41 +488,41 @@
     from_east = lax.ppermute(to_west, "lon", to_prev)
     from_west = lax.ppermute(to_east, "lon", to_next)
 
-    groups = weights.shape[0] // GROUP
-    coupling_scratch = [
-        pltpu.VMEM((slots, 4 * BLOCK), bf16),
-        pltpu.VMEM((slots, BLOCK), bf16),
-        pltpu.VMEM((2, slots, 2 * BLOCK), f32),
-        pltpu.VMEM((groups, GROUP, BLOCK, BLOCK), f32),
-        pltpu.SemaphoreType.DMA((groups,)),
-    ]
-    coupling_flops = 4 * slots * weights.shape[0] * 4 * BLOCK * BLOCK * 2
+    blocks_of, atm = weights.shape[0], atm_state.shape[2]
+    groups = blocks_of // GROUP
     sum_parts = 2 * halves + 1
-    (sums,) = call(
+    ocean_blocks = lon_count * halves * tile_lat
+    held_rows = -(-places(slots, blocks_of) * blocks_of // BLOCK) * BLOCK
+
+    def coupling_scratch(result_rows):
+        return [
+            pltpu.VMEM((result_rows, 2 * BLOCK), f32),
+            pltpu.VMEM((held_rows, BLOCK), f32),
+            pltpu.VMEM((held_rows, 4 * BLOCK), f32),
+            pltpu.VMEM((held_rows, 2 * BLOCK), f32),
+            pltpu.VMEM((groups, GROUP, BLOCK, BLOCK), f32),
+            pltpu.SemaphoreType.DMA((groups,)),
+        ]
+
+    coupling_flops = 4 * slots * blocks_of * 2 * BLOCK * BLOCK * 2
+    sums, rank = call(
         weigh,
-        [(lon_count, sum_parts, tile_lat, BLOCK)],
-        [*coupling_scratch, in_vmem(atm_state), in_vmem(margins), pltpu.SemaphoreType.DMA((2,))],
+        [(lon_count, sum_parts, tile_lat, BLOCK), (1, slots)],
+        [*coupling_scratch(ocean_blocks), in_vmem(atm_state), in_vmem(margins), pltpu.SemaphoreType.DMA((2,))],
         coupling_flops,
         name="weigh",
         inputs=4,
         far=range(3),
     )(atm_state, margins, weights, to_west)
-
-    sources = count * halves + 2 * parts + lon_count * sum_parts
+    received = lax.all_to_all(sums, "lon", split_axis=0, concat_axis=0, tiled=True)
+
+    sources = count * halves + 2 * parts
     message = (-(-sources // 2), 8, BLOCK)
-    to_north, to_south = call(pack_rows, [message, message], name="pack_rows", inputs=4)(
-        fields, from_west, from_east, sums
+    to_north, to_south = call(pack_rows, [message, message], name="pack_rows", inputs=3)(
+        fields, from_west, from_east
     )
     from_south = lax.ppermute(to_north, "lat", up)
     from_north = lax.ppermute(to_south, "lat", down)
-
-    (payload,) = call(
-        functools.partial(place_sums, sources - lon_count * sum_parts),
-        [(lon_count, sum_parts, tile_lat + 8, BLOCK)],
-        name="place_sums",
-        inputs=3,
-    )(sums, from_north, from_south)
-    received = lax.all_to_all(payload, "lon", split_axis=0, concat_axis=0, tiled=True)
 
     wide = (tile_lat + 8, tile_lon + BLOCK)
     adjoint, blocks, coeffs, start = call(
@@ -494,23 +539,29 @@
     )(fields, from_west, from_east, from_north, from_south)
     gathered = lax.all_to_all(blocks, "lon", split_axis=0, concat_axis=0, tiled=True)
 
+    message = (8, tile_lon + BLOCK)
+    forcing, to_north, to_south = call(
+        sum_forcing, [(2, tile_lat, tile_lon + BLOCK), message, message], name="sum_forcing", inputs=1
+    )(received)
+    force_south = lax.ppermute(to_north, "lat", up)
+    force_north = lax.ppermute(to_south, "lat", down)
     (final,) = call(
         run_forward,
         [tracers.shape],
         [pltpu.VMEM((2, levels, *wide), f32)],
         name="run_forward",
-        inputs=3,
-    )(coeffs, start, received)
+        inputs=5,
+    )(coeffs, start, forcing, force_north, force_south)
 
     (gradient,) = call(
         unweigh,
         [atm_state.shape],
-        [*coupling_scratch, in_vmem(margins), pltpu.SemaphoreType.DMA((1,))],
+        [*coupling_scratch(atm), in_vmem(margins), pltpu.SemaphoreType.DMA((1,))],
         coupling_flops,
         name="unweigh",
-        inputs=3,
-        far=(1, 2),
-    )(gathered, margins, weights)
+        inputs=4,
+        far=(2, 3),
+    )(gathered, rank, margins, weights)
     return (final, adjoint, gradient)
 
 

time: 60.7 us -> 54.7 us (0.901)
  the two profiles are of different devices: /device:TPU:0 before, /device:TPU:1 now
where the time goes in v1:
time: 54.7 us; the launch traced here: 54.1 us
  starting transfers between devices  27.7 us (51%)
  Pallas kernels  17.3 us (32%)
  waiting for transfers between devices  8.45 us (15%)
  between operations  0.7 us (1%)
    pallas_call x7, Pallas kernels, run(): kernel(*(pltpu.with_memory_space_constraint(x, pltpu.HBM) if n in far els...  17.3 us
    all_to_all x1, starting transfers between devices, on_device(): lax.all_to_all(sums, 'lon', split_axis=0, concat_axis=0, tiled=True)  6.36 us
    ppermute x1, waiting for transfers between devices, on_device(): from_west = lax.ppermute(to_east, 'lon', to_next)  4.51 us
    ppermute x1, starting transfers between devices, on_device(): from_north = lax.ppermute(to_south, 'lat', down)  4.42 us
    ppermute x1, starting transfers between devices, on_device(): force_south = lax.ppermute(to_north, 'lat', up)  4.38 us
    ppermute x1, starting transfers between devices, on_device(): from_east = lax.ppermute(to_west, 'lon', to_prev)  4.16 us
    all_to_all x1, starting transfers between devices, on_device(): lax.all_to_all(blocks, 'lon', split_axis=0, concat_axis=0, tiled=True)  3.41 us
    ppermute x1, starting transfers between devices, on_device(): from_south = lax.ppermute(to_north, 'lat', up)  3.06 us
  transfers between devices with their start and end apart: 8, of which 5 were waited for; matrix products, arithmetic and copies ran while one was open for 0% of the time, Pallas kernels for 8%

profile of v1, /device:TPU:1, one launch (start us, length us, event | category | flops | bytes accessed | tf_op | source)
XLA Modules:
  0.0 54.1 jit_solution(4556096198897460100)
XLA Ops:
  0.6 1.4 %pack_columns.1 = (f32[35,16,256]{2,1,0:T(8,128)S(1)}, f32[2,16,128]{2,1,0:T(8,128)S(1)}, f32[2,16,128]{2,1,0:T(8,128)S(1)}) custom-call(f32[2,4,16,256]{3,2,1,0:T(8,128)} %refs_0_.1, f32[2,4,16,256]{3,2,1,0:T(8,128)} %refs_1_.1, s32[4,16,256]{2,1,0:T(8,128)} %refs_2_.1, f32[3,4,16,256]{3,2,1,0:T(8,128)} %refs_3_.1, f32[2,4,16,256]{3,2,1,0:T(8,128)} %refs_4_.1), custom_call_target="tpu_custom_call" | custom-call | bytes 1048576 | tf_op jit(solution)/shard_map/pack_columns/pallas_call | solution.py:33
  2.1 6.2 %weigh.1 = (f32[8,5,16,128]{3,2,1,0:T(8,128)}, f32[1,512]{1,0:T(1,128)S(1)}) custom-call(f32[2,1,256,128]{3,2,1,0:T(8,128)} %atm_state.1, s32[3,1,1,8,64]{4,3,2,1,0:T(8,128)} %margins.3, f32[32,128,128]{2,1,0:T(8,128)} %weights.3, f32[2,16,128]{2,1,0:T(8,128)S(1)} %get-tuple-element.19.after), custom_call_target="tpu_custom_call" | custom-call | flops 4294967296 | bytes 1048576 | tf_op jit(solution)/shard_map/weigh/pallas_call | solution.py:33
  8.3 6.4 %all-to-all-start = ((f32[8,5,16,128]{3,2,1,0:T(8,128)}), f32[8,5,16,128]{3,2,1,0:T(8,128)S(1)}, u32[]{:S(2)}, u32[]{:S(2)}) async-start(f32[8,5,16,128]{3,2,1,0:T(8,128)} %get-tuple-element.24), calls=%async_computation | async-start | bytes 655360 | tf_op jit(solution)/shard_map/all_to_all | solution.py:517
  14.7 4.2 %collective-permute-start.1 = (f32[2,16,128]{2,1,0:T(8,128)S(1)}, f32[2,16,128]{2,1,0:T(8,128)S(1)}, u32[]{:S(2)}, u32[]{:S(2)}) collective-permute-start(f32[2,16,128]{2,1,0:T(8,128)S(1)} %get-tuple-element.19.after), channel_id=1, source_target_pairs={{1,0},{2,1},{3,2},{4,3},{5,4},{6,5},{7,6},{0,7},{9,8},{10,9},{11,1... | collective-permute-start | bytes 49160 | tf_op jit(solution)/shard_map/ppermute | solution.py:488
  18.8 0.0 collective-permute-start
  18.8 1.0 %collective-permute-done.1.from_east = f32[2,16,128]{2,1,0:T(8,128)S(1)} collective-permute-done((f32[2,16,128]{2,1,0:T(8,128)S(1)}, f32[2,16,128]{2,1,0:T(8,128)S(1)}, u32[]{:S(2)}, u32[]{:S(2)}) %collective-permute-start.1) | collective-permute-done | bytes 16416 | tf_op jit(solution)/shard_map/ppermute | solution.py:488
  19.9 4.5 %collective-permute-done.from_west = f32[2,16,128]{2,1,0:T(8,128)S(1)} collective-permute-done((f32[2,16,128]{2,1,0:T(8,128)S(1)}, f32[2,16,128]{2,1,0:T(8,128)S(1)}, u32[]{:S(2)}, u32[]{:S(2)}) %collective-permute-start) | collective-permute-done | bytes 16416 | tf_op jit(solution)/shard_map/ppermute | solution.py:489
  24.4 4.4 %collective-permute-start.2 = (f32[37,8,128]{2,1,0:T(8,128)S(1)}, f32[37,8,128]{2,1,0:T(8,128)S(1)}, u32[]{:S(2)}, u32[]{:S(2)}) collective-permute-start(f32[37,8,128]{2,1,0:T(8,128)S(1)} %get-tuple-element.20), channel_id=1, source_target_pairs={{8,0},{16,8},{24,16},{9,1},{17,9},{25,17},{10,2},{18,10},{26,18},{... | collective-permute-start | bytes 454664 | tf_op jit(solution)/shard_map/ppermute | solution.py:525
  28.8 3.1 %collective-permute-start.3 = (f32[37,8,128]{2,1,0:T(8,128)S(1)}, f32[37,8,128]{2,1,0:T(8,128)S(1)}, u32[]{:S(2)}, u32[]{:S(2)}) collective-permute-start(f32[37,8,128]{2,1,0:T(8,128)S(1)} %get-tuple-element.21), channel_id=1, source_target_pairs={{0,8},{8,16},{16,24},{1,9},{9,17},{17,25},{2,10},{10,18},{18,26},{... | collective-permute-start | bytes 454664 | tf_op jit(solution)/shard_map/ppermute | solution.py:524
  31.9 0.9 %collective-permute-done.2.from_north = f32[37,8,128]{2,1,0:T(8,128)S(1)} collective-permute-done((f32[37,8,128]{2,1,0:T(8,128)S(1)}, f32[37,8,128]{2,1,0:T(8,128)S(1)}, u32[]{:S(2)}, u32[]{:S(2)}) %collective-permute-start.2) | collective-permute-done | bytes 151584 | tf_op jit(solution)/shard_map/ppermute | solution.py:525
  32.8 1.2 %collective-permute-done.3.from_south = f32[37,8,128]{2,1,0:T(8,128)S(1)} collective-permute-done((f32[37,8,128]{2,1,0:T(8,128)S(1)}, f32[37,8,128]{2,1,0:T(8,128)S(1)}, u32[]{:S(2)}, u32[]{:S(2)}) %collective-permute-start.3) | collective-permute-done | bytes 151584 | tf_op jit(solution)/shard_map/ppermute | solution.py:524
  34.0 2.4 %run_adjoint.1 = (f32[2,4,16,256]{3,2,1,0:T(8,128)}, f32[8,64,128]{2,1,0:T(8,128)}, f32[6,4,24,384]{3,2,1,0:T(8,128)S(1)}, f32[2,4,24,384]{3,2,1,0:T(8,128)S(1)}) custom-call(f32[35,16,256]{2,1,0:T(8,128)S(1)} %get-tuple-element.17.fields, f32[2,16,128]{2,1,0:T(8,128)S(1)} %collective-permute-done.from_west, ...), custom_call_target="tpu_custom_call" | custom-call | bytes 1048576 | tf_op jit(solution)/shard_map/run_adjoint/pallas_call | solution.py:33
  36.5 0.0 all-to-all-done.received
  36.5 3.4 %all-to-all-start.1 = ((f32[8,64,128]{2,1,0:T(8,128)}), f32[8,64,128]{2,1,0:T(8,128)S(1)}, u32[]{:S(2)}, u32[]{:S(2)}) async-start(f32[8,64,128]{2,1,0:T(8,128)} %get-tuple-element.29), calls=%async_computation.1 | async-start | bytes 524288 | tf_op jit(solution)/shard_map/all_to_all | solution.py:540
  39.9 0.1 sum_forcing.1
  40.0 1.9 %collective-permute-start.4 = (f32[8,384]{1,0:T(8,128)S(1)}, f32[8,384]{1,0:T(8,128)S(1)}, u32[]{:S(2)}, u32[]{:S(2)}) collective-permute-start(f32[8,384]{1,0:T(8,128)S(1)} %get-tuple-element.26), channel_id=1, source_target_pairs={{8,0},{16,8},{24,16},{9,1},{17,9},{25,17},{10,2},{18,10},{26,18},{... | collective-permute-start | bytes 36872 | tf_op jit(solution)/shard_map/ppermute | solution.py:547
  41.9 4.4 %collective-permute-start.5 = (f32[8,384]{1,0:T(8,128)S(1)}, f32[8,384]{1,0:T(8,128)S(1)}, u32[]{:S(2)}, u32[]{:S(2)}) collective-permute-start(f32[8,384]{1,0:T(8,128)S(1)} %get-tuple-element.27), channel_id=1, source_target_pairs={{0,8},{8,16},{16,24},{1,9},{9,17},{17,25},{2,10},{10,18},{18,26},{... | collective-permute-start | bytes 36872 | tf_op jit(solution)/shard_map/ppermute | solution.py:546
  46.3 0.0 collective-permute-done.4.from_north
  46.3 0.8 %collective-permute-done.5.from_south = f32[8,384]{1,0:T(8,128)S(1)} collective-permute-done((f32[8,384]{1,0:T(8,128)S(1)}, f32[8,384]{1,0:T(8,128)S(1)}, u32[]{:S(2)}, u32[]{:S(2)}) %collective-permute-start.5) | collective-permute-done | bytes 12320 | tf_op jit(solution)/shard_map/ppermute | solution.py:546
  47.1 1.6 %run_forward.1 = f32[2,4,16,256]{3,2,1,0:T(8,128)} custom-call(f32[6,4,24,384]{3,2,1,0:T(8,128)S(1)} %get-tuple-element.22.coeffs, f32[2,4,24,384]{3,2,1,0:T(8,128)S(1)} %get-tuple-element.23.start, f32[2,16,384]{2,1,0:T(8,128)S(1)} %get-tuple-element.25.forcing, f32[8,384]{1,0:T(8,128)S(1)} %collective-permute-done.4.from_north, ...), custom_call_target="tpu_custom_call" | custom-call | bytes 1048576 | tf_op jit(solution)/shard_map/run_forward/pallas_call | solution.py:33
  48.7 0.0 all-to-all-done.1.gathered
  48.7 5.5 %unweigh.1 = f32[2,1,256,128]{3,2,1,0:T(8,128)} custom-call(f32[8,64,128]{2,1,0:T(8,128)S(1)} %all-to-all-done.1.gathered, f32[1,512]{1,0:T(1,128)S(1)} %get-tuple-element.30.rank, s32[3,1,1,8,64]{4,3,2,1,0:T(8,128)} %margins.3, f32[32,128,128]{2,1,0:T(8,128)} %weights.3), custom_call_target="tpu_custom_call" | custom-call | flops 4294967296 | bytes 1048576 | tf_op jit(solution)/shard_map/unweigh/pallas_call | solution.py:33
  (1 shorter events, 0.0 us)
Async XLA Ops:
  8.3 28.2 %all-to-all-start = ((f32[8,5,16,128]{3,2,1,0:T(8,128)}), f32[8,5,16,128]{3,2,1,0:T(8,128)S(1)}, u32[]{:S(2)}, u32[]{:S(2)}) async-start(f32[8,5,16,128]{3,2,1,0:T(8,128)} %get-tuple-element.24), calls=%async_computation | async-start | bytes 655360 | tf_op jit(solution)/shard_map/all_to_all | solution.py:517
  14.7 5.2 %collective-permute-start.1 = (f32[2,16,128]{2,1,0:T(8,128)S(1)}, f32[2,16,128]{2,1,0:T(8,128)S(1)}, u32[]{:S(2)}, u32[]{:S(2)}) collective-permute-start(f32[2,16,128]{2,1,0:T(8,128)S(1)} %get-tuple-element.19.after), channel_id=1, source_target_pairs={{1,0},{2,1},{3,2},{4,3},{5,4},{6,5},{7,6},{0,7},{9,8},{10,9},{11,1... | collective-permute-start | bytes 49160 | tf_op jit(solution)/shard_map/ppermute | solution.py:488
  18.8 5.5 %collective-permute-start = (f32[2,16,128]{2,1,0:T(8,128)S(1)}, f32[2,16,128]{2,1,0:T(8,128)S(1)}, u32[]{:S(2)}, u32[]{:S(2)}) collective-permute-start(f32[2,16,128]{2,1,0:T(8,128)S(1)} %get-tuple-element.18), channel_id=1, source_target_pairs={{0,1},{1,2},{2,3},{3,4},{4,5},{5,6},{6,7},{7,0},{8,9},{9,10},{10,1... | collective-permute-start | bytes 49160 | tf_op jit(solution)/shard_map/ppermute | solution.py:489
  24.4 8.4 %collective-permute-start.2 = (f32[37,8,128]{2,1,0:T(8,128)S(1)}, f32[37,8,128]{2,1,0:T(8,128)S(1)}, u32[]{:S(2)}, u32[]{:S(2)}) collective-permute-start(f32[37,8,128]{2,1,0:T(8,128)S(1)} %get-tuple-element.20), channel_id=1, source_target_pairs={{8,0},{16,8},{24,16},{9,1},{17,9},{25,17},{10,2},{18,10},{26,18},{... | collective-permute-start | bytes 454664 | tf_op jit(solution)/shard_map/ppermute | solution.py:525
  28.8 5.2 %collective-permute-start.3 = (f32[37,8,128]{2,1,0:T(8,128)S(1)}, f32[37,8,128]{2,1,0:T(8,128)S(1)}, u32[]{:S(2)}, u32[]{:S(2)}) collective-permute-start(f32[37,8,128]{2,1,0:T(8,128)S(1)} %get-tuple-element.21), channel_id=1, source_target_pairs={{0,8},{8,16},{16,24},{1,9},{9,17},{17,25},{2,10},{10,18},{18,26},{... | collective-permute-start | bytes 454664 | tf_op jit(solution)/shard_map/ppermute | solution.py:524
  36.5 12.2 %all-to-all-start.1 = ((f32[8,64,128]{2,1,0:T(8,128)}), f32[8,64,128]{2,1,0:T(8,128)S(1)}, u32[]{:S(2)}, u32[]{:S(2)}) async-start(f32[8,64,128]{2,1,0:T(8,128)} %get-tuple-element.29), calls=%async_computation.1 | async-start | bytes 524288 | tf_op jit(solution)/shard_map/all_to_all | solution.py:540
  40.0 6.3 %collective-permute-start.4 = (f32[8,384]{1,0:T(8,128)S(1)}, f32[8,384]{1,0:T(8,128)S(1)}, u32[]{:S(2)}, u32[]{:S(2)}) collective-permute-start(f32[8,384]{1,0:T(8,128)S(1)} %get-tuple-element.26), channel_id=1, source_target_pairs={{8,0},{16,8},{24,16},{9,1},{17,9},{25,17},{10,2},{18,10},{26,18},{... | collective-permute-start | bytes 36872 | tf_op jit(solution)/shard_map/ppermute | solution.py:547
  41.9 5.2 %collective-permute-start.5 = (f32[8,384]{1,0:T(8,128)S(1)}, f32[8,384]{1,0:T(8,128)S(1)}, u32[]{:S(2)}, u32[]{:S(2)}) collective-permute-start(f32[8,384]{1,0:T(8,128)S(1)} %get-tuple-element.27), channel_id=1, source_target_pairs={{0,8},{8,16},{16,24},{1,9},{9,17},{17,25},{2,10},{10,18},{18,26},{... | collective-permute-start | bytes 36872 | tf_op jit(solution)/shard_map/ppermute | solution.py:546

commit v2 on v1

--- a/solution.py
+++ b/solution.py
@@ -9,20 +9,31 @@
 STEPS = 4
 HALO = STEPS
 PER_LANES = BLOCK // HALO
-GROUP = 4
+GROUP = 8
 f32 = jnp.float32
 bf16 = jnp.bfloat16
 VMEM_LIMIT = 48 * 1024 * 1024
 
 
-def call(body, outs, scratch=(), flops=0, name=None, inputs=0, far=()):
+def call(body, outs, scratch=(), flops=0, name=None, inputs=0, far=(), aliases=None):
     outs = [s if isinstance(s, jax.ShapeDtypeStruct) else jax.ShapeDtypeStruct(s, f32) for s in outs]
     near = pl.BlockSpec(memory_space=pltpu.VMEM)
+    aliases = aliases or {}
     kernel = pl.pallas_call(
         body,
         out_shape=outs,
-        in_specs=[pl.BlockSpec(memory_space=pltpu.HBM) if n in far else near for n in range(inputs)],
-        out_specs=[near] * len(outs),
+        in_specs=[
+            pl.BlockSpec(memory_space=pl.ANY)
+            if n in aliases
+            else pl.BlockSpec(memory_space=pltpu.HBM)
+            if n in far
+            else near
+            for n in range(inputs)
+        ],
+        out_specs=[
+            pl.BlockSpec(memory_space=pl.ANY) if n in aliases.values() else near for n in range(len(outs))
+        ],
+        input_output_aliases=aliases,
         scratch_shapes=list(scratch),
         compiler_params=pltpu.CompilerParams(vmem_limit_bytes=VMEM_LIMIT),
         cost_estimate=pl.CostEstimate(flops=flops, bytes_accessed=1 << 20, transcendentals=0),
@@ -71,8 +82,9 @@
 
 
 def pack_columns(*refs):
-    inputs, (fields, to_west, to_east), scratch = refs[:5], refs[5:8], refs[8:]
-    for copy in fetch(zip(inputs, scratch[:5]), scratch[5]):
+    inputs, (fields, to_west, to_east), scratch = refs[:7], refs[7:10], refs[12:]
+    copies = fetch(zip(inputs, [*scratch[:5], *refs[10:12]]), scratch[5])
+    for copy in copies[:5]:
         copy.wait()
     shape = to_west.shape[1:]
     lane = lanes(shape)
@@ -88,6 +100,8 @@
     for part in range(to_west.shape[0]):
         to_west[part] = west[part]
         to_east[part] = east[part]
+    for copy in copies[5:]:
+        copy.wait()
 
 
 def unpack_columns(from_west, from_east, i):
@@ -107,7 +121,7 @@
     return out
 
 
-def pack_rows(fields, from_west, from_east, to_north, to_south):
+def pack_rows(fields, from_west, from_east, sums, to_north, to_south, same_sums):
     sources = [ref[at] for ref, at in row_sources(fields, from_west, from_east)]
     half = to_north.shape[0]
     row = rows((8, BLOCK))
@@ -313,25 +327,27 @@
     return jnp.sum(jnp.where(mine, before, 0.0), axis=0, keepdims=True)
 
 
-def couple(weights_near, ready, table, keys, block_row, rank, gather_first, transposed, result, scratch):
-    code, size = keys
-    column, vectors, products = scratch
+def find_slots(r, code, block_row, rank, capacity, column):
     slots = block_row.shape[1]
-    blocks = weights_near.shape[0] * weights_near.shape[1]
-    capacity = places(slots, blocks)
+    place = rank.astype(jnp.int32) - r * capacity
+    place = jnp.where((place >= 0) & (place < capacity), block_row * capacity + place, -1)
+    for at in range(0, column.shape[0], BLOCK):
+        here = rows((BLOCK, slots)) + at == place
+        found = jnp.sum(jnp.where(here, code + 1.0, 0.0), axis=1, keepdims=True) - 1.0
+        column[at : at + BLOCK] = jnp.broadcast_to(found, (BLOCK, BLOCK))
+
+
+def couple(weights_near, table, size, capacity, rounds, prepare, column, gather_first, transposed, result, scratch):
+    vectors, products = scratch
     total_rows = column.shape[0]
     result[...] = jnp.zeros_like(result)
-    rounds = jnp.max(rank).astype(jnp.int32) // capacity + 1
 
     def one_round(r, carry):
-        place = rank.astype(jnp.int32) - r * capacity
-        place = jnp.where((place >= 0) & (place < capacity), block_row * capacity + place, -1)
+        prepare(r)
         eye = rows((BLOCK, BLOCK)) == lanes((BLOCK, BLOCK))
         place_hot = []
         for at in range(0, total_rows, BLOCK):
-            here = rows((BLOCK, slots)) + at == place
-            found = jnp.sum(jnp.where(here, code + 1.0, 0.0), axis=1, keepdims=True) - 1.0
-            found = jnp.broadcast_to(found, (BLOCK, BLOCK))
+            found = column[at : at + BLOCK]
             first = jnp.floor((found + 0.5) * (1.0 / size))
             second = found - first * size
             gather, put = (first, second) if gather_first else (second, first)
@@ -341,7 +357,6 @@
             vectors[at : at + BLOCK] = jnp.dot(hot, table, preferred_element_type=f32)
             put = jnp.sum(jnp.where(eye, put, 0.0), axis=0, keepdims=True)
             place_hot.append(one_hot(rows((result.shape[0], BLOCK)).astype(f32) == put))
-        pl.when(r == 0)(ready)
 
         def group(g, carry):
             for u in range(GROUP):
@@ -380,32 +395,28 @@
     return as_row((order * atm + atm_ids).astype(f32)), as_row(block_ids)
 
 
-def weigh(atm_state, margins, weights, after, sums, rank_out, result, *scratch):
-    scratch, (held, arrived, atm_near, ids, near) = scratch[:3], scratch[3:]
+def weigh(atm_near, margins, weights, after, sums, found, keys, result, *scratch):
+    scratch, (held, arrived) = scratch[:2], scratch[2:]
+    fetch_weights(weights, held, arrived)
     lon_count = margins.shape[3]
-    atm = atm_state.shape[2]
+    atm = atm_near.shape[2]
+    blocks = weights.shape[0]
     tile_lat = sums.shape[2]
-    copies = fetch([(margins, ids), (atm_state, atm_near)], near)
-    fetch_weights(weights, held, arrived)
-    for copy in copies:
-        copy.wait()
-    code, block_row = slot_keys(ids, tile_lat, atm)
-    rank = rank_slots(block_row, weights.shape[0])
-    rank_out[...] = rank
+    code, block_row = slot_keys(margins, tile_lat, atm)
+    rank = rank_slots(block_row, blocks)
+    keys[0:1] = code
+    keys[1:2] = block_row.astype(f32)
+    keys[2:3] = rank
+    capacity = places(code.shape[1], blocks)
+    rounds = jnp.max(rank).astype(jnp.int32) // capacity + 1
     parts = [split(atm_near[f, 0]) for f in range(2)]
     table = jnp.concatenate([parts[f][n] for n in range(2) for f in range(2)], axis=1)
-    couple(
-        held,
-        lambda: wait_weights(weights, held, arrived),
-        table,
-        (code, atm),
-        block_row,
-        rank,
-        False,
-        False,
-        result,
-        scratch,
-    )
+
+    def prepare(r):
+        find_slots(rounds - 1 - r, code, block_row, rank, capacity, found)
+        pl.when(r == 0)(lambda: wait_weights(weights, held, arrived))
+
+    couple(held, table, atm, capacity, rounds, prepare, found, False, False, result, scratch)
     lane = lanes((tile_lat, BLOCK))
 
     def block_sums(k, f, h):
@@ -426,15 +437,14 @@
         sums[k, 4] = edge
 
 
-def unweigh(gathered, rank, margins, weights, gradient, result, *scratch):
-    scratch, (held, arrived, ids, near) = scratch[:3], scratch[3:]
+def unweigh(gathered, found, keys, weights, gradient, result, column, *scratch):
+    scratch, (held, arrived) = scratch[:2], scratch[2:]
+    fetch_weights(weights, held, arrived)
     atm = gradient.shape[2]
+    blocks = weights.shape[0]
     lon_count, ocean_blocks = gathered.shape[0], gathered.shape[1] // 2
-    copies = fetch([(margins, ids)], near)
-    fetch_weights(weights, held, arrived)
-    for copy in copies:
-        copy.wait()
-    code, block_row = slot_keys(ids, ocean_blocks // 2, atm)
+    capacity = places(keys.shape[1], blocks)
+    rounds = jnp.max(keys[2:3]).astype(jnp.int32) // capacity + 1
     parts = [
         split(
             jnp.concatenate(
@@ -444,18 +454,18 @@
         for f in range(2)
     ]
     table = jnp.concatenate([parts[f][n] for n in range(2) for f in range(2)], axis=1)
-    couple(
-        held,
-        lambda: wait_weights(weights, held, arrived),
-        table,
-        (code, atm),
-        block_row,
-        rank[...],
-        True,
-        True,
-        result,
-        scratch,
-    )
+
+    def prepare(r):
+        @pl.when(r == 0)
+        def _():
+            column[...] = found[...]
+            wait_weights(weights, held, arrived)
+
+        @pl.when(r > 0)
+        def _():
+            find_slots(r, keys[0:1], keys[1:2].astype(jnp.int32), keys[2:3], capacity, column)
+
+    couple(held, table, atm, capacity, rounds, prepare, column, True, True, result, scratch)
     for f in range(2):
         gradient[f, 0] = result[:, f * BLOCK : (f + 1) * BLOCK]
 
@@ -477,14 +487,20 @@
         return pltpu.VMEM(s.shape, s.dtype)
 
     message = (parts, tile_lat, BLOCK)
-    fields, to_west, to_east = call(
+    fields, to_west, to_east, atm_near, margins_near = call(
         pack_columns,
-        [(count, tile_lat, tile_lon), message, message],
-        [*map(in_vmem, inputs), pltpu.SemaphoreType.DMA((5,))],
+        [
+            (count, tile_lat, tile_lon),
+            message,
+            message,
+            atm_state.shape,
+            jax.ShapeDtypeStruct(margins.shape, margins.dtype),
+        ],
+        [*map(in_vmem, inputs), pltpu.SemaphoreType.DMA((7,))],
         name="pack_columns",
-        inputs=5,
-        far=range(5),
-    )(*inputs)
+        inputs=7,
+        far=range(7),
+    )(*inputs, atm_state, margins)
     from_east = lax.ppermute(to_west, "lon", to_prev)
     from_west = lax.ppermute(to_east, "lon", to_next)
 
@@ -497,7 +513,6 @@
     def coupling_scratch(result_rows):
         return [
             pltpu.VMEM((result_rows, 2 * BLOCK), f32),
-            pltpu.VMEM((held_rows, BLOCK), f32),
             pltpu.VMEM((held_rows, 4 * BLOCK), f32),
             pltpu.VMEM((held_rows, 2 * BLOCK), f32),
             pltpu.VMEM((groups, GROUP, BLOCK, BLOCK), f32),
@@ -505,22 +520,22 @@
         ]
 
     coupling_flops = 4 * slots * blocks_of * 2 * BLOCK * BLOCK * 2
-    sums, rank = call(
+    sums, found, keys = call(
         weigh,
-        [(lon_count, sum_parts, tile_lat, BLOCK), (1, slots)],
-        [*coupling_scratch(ocean_blocks), in_vmem(atm_state), in_vmem(margins), pltpu.SemaphoreType.DMA((2,))],
+        [(lon_count, sum_parts, tile_lat, BLOCK), (held_rows, BLOCK), (8, slots)],
+        coupling_scratch(ocean_blocks),
         coupling_flops,
         name="weigh",
         inputs=4,
-        far=range(3),
-    )(atm_state, margins, weights, to_west)
-    received = lax.all_to_all(sums, "lon", split_axis=0, concat_axis=0, tiled=True)
+        far=(2,),
+    )(atm_near, margins_near, weights, to_west)
 
     sources = count * halves + 2 * parts
     message = (-(-sources // 2), 8, BLOCK)
-    to_north, to_south = call(pack_rows, [message, message], name="pack_rows", inputs=3)(
-        fields, from_west, from_east
-    )
+    to_north, to_south, sums = call(
+        pack_rows, [message, message, sums.shape], name="pack_rows", inputs=4, aliases={3: 2}
+    )(fields, from_west, from_east, sums)
+    received = lax.all_to_all(sums, "lon", split_axis=0, concat_axis=0, tiled=True)
     from_south = lax.ppermute(to_north, "lat", up)
     from_north = lax.ppermute(to_south, "lat", down)
 
@@ -556,12 +571,12 @@
     (gradient,) = call(
         unweigh,
         [atm_state.shape],
-        [*coupling_scratch(atm), in_vmem(margins), pltpu.SemaphoreType.DMA((1,))],
+        [coupling_scratch(atm)[0], in_vmem(found), *coupling_scratch(atm)[1:]],
         coupling_flops,
         name="unweigh",
         inputs=4,
-        far=(2, 3),
-    )(gathered, rank, margins, weights)
+        far=(3,),
+    )(gathered, found, keys, weights)
     return (final, adjoint, gradient)
 
 

time: 54.7 us -> 46.2 us (0.84)
  waiting for transfers between devices: 8.45 us -> 2.93 us
  Pallas kernels: 17.3 us -> 15 us
  starting transfers between devices: 27.7 us -> 26.9 us
    ppermute x1, waiting for transfers between devices: 4.51 us -> 0.01 us  [on_device(): from_west = lax.ppermute(to_east, 'lon', to_next)]
    all_to_all x1, starting transfers between devices: 6.36 us -> 3.44 us  [on_device(): lax.all_to_all(sums, 'lon', split_axis=0, concat_axis=0, tiled=True)]
    pallas_call x7, Pallas kernels: 17.3 us -> 15 us  [run(): kernel(*(pltpu.with_memory_space_constraint(x, pltpu.HBM) if n in far els...]
    all_to_all x1, starting transfers between devices: 3.41 us -> 5.64 us  [on_device(): lax.all_to_all(blocks, 'lon', split_axis=0, concat_axis=0, tiled=True)]
    ppermute x1, starting transfers between devices: 0.01 us -> 2.09 us  [on_device(): from_west = lax.ppermute(to_east, 'lon', to_next)]
    ppermute x1, starting transfers between devices: 4.42 us -> 2.87 us  [on_device(): from_north = lax.ppermute(to_south, 'lat', down)]
    ppermute x1, starting transfers between devices: 4.16 us -> 3.1 us  [on_device(): from_east = lax.ppermute(to_west, 'lon', to_prev)]
    ppermute x1, waiting for transfers between devices: 1.02 us -> 0.01 us  [on_device(): from_east = lax.ppermute(to_west, 'lon', to_prev)]
  transfers between devices with their start and end apart: 8 -> 8, of which waited for: 5 -> 3; matrix products, arithmetic and copies ran while one was open for 0% -> 0% of each run, Pallas kernels for 8% -> 20%
where the time goes in v2:
time: 46.2 us; the launch traced here: 45.5 us
  starting transfers between devices  26.9 us (58%)
  Pallas kernels  15 us (32%)
  waiting for transfers between devices  2.93 us (6%)
  between operations  0.73 us (2%)
    pallas_call x7, Pallas kernels, run(): kernel(*(pltpu.with_memory_space_constraint(x, pltpu.HBM) if n in far els...  15 us
    all_to_all x1, starting transfers between devices, on_device(): lax.all_to_all(blocks, 'lon', split_axis=0, concat_axis=0, tiled=True)  5.64 us
    ppermute x1, starting transfers between devices, on_device(): force_south = lax.ppermute(to_north, 'lat', up)  4.66 us
    all_to_all x1, starting transfers between devices, on_device(): lax.all_to_all(sums, 'lon', split_axis=0, concat_axis=0, tiled=True)  3.44 us
    ppermute x1, starting transfers between devices, on_device(): from_south = lax.ppermute(to_north, 'lat', up)  3.17 us
    ppermute x1, starting transfers between devices, on_device(): from_east = lax.ppermute(to_west, 'lon', to_prev)  3.1 us
    ppermute x1, starting transfers between devices, on_device(): from_north = lax.ppermute(to_south, 'lat', down)  2.87 us
    ppermute x1, starting transfers between devices, on_device(): from_west = lax.ppermute(to_east, 'lon', to_next)  2.09 us
  transfers between devices with their start and end apart: 8, of which 3 were waited for; matrix products, arithmetic and copies ran while one was open for 0% of the time, Pallas kernels for 20%

profile of v2, /device:TPU:1, one launch (start us, length us, event | category | flops | bytes accessed | tf_op | source)
XLA Modules:
  0.0 45.5 jit_solution(2289577397919300936)
XLA Ops:
  0.6 1.4 %pack_columns.1 = (f32[35,16,256]{2,1,0:T(8,128)S(1)}, f32[2,16,128]{2,1,0:T(8,128)S(1)}, f32[2,16,128]{2,1,0:T(8,128)S(1)}, f32[2,1,256,128]{3,2,1,0:T(8,128)S(1)}, s32[3,1,1,8,64]{4,3,2,1,0:T(8,128)S(1)}) custom-call(f32[2,4,16,256]{3,2,1,0:T(8,128)} %refs_0_.1, f32[2,4,16,256]{3,2,1,0:T(8,128)} %refs_1_.1, s32[4,16,256]{2,1,0:T(8,128)} %refs_2_.1, ...), custom_call_target="tpu_custom_call" | custom-call | bytes 1048576 | tf_op jit(solution)/shard_map/pack_columns/pallas_call | solution.py:44
  2.1 2.1 %collective-permute-start = (f32[2,16,128]{2,1,0:T(8,128)S(1)}, f32[2,16,128]{2,1,0:T(8,128)S(1)}, u32[]{:S(2)}, u32[]{:S(2)}) collective-permute-start(f32[2,16,128]{2,1,0:T(8,128)S(1)} %get-tuple-element.22), channel_id=1, source_target_pairs={{0,1},{1,2},{2,3},{3,4},{4,5},{5,6},{6,7},{7,0},{8,9},{9,10},{10,1... | collective-permute-start | bytes 49160 | tf_op jit(solution)/shard_map/ppermute | solution.py:505
  4.2 3.1 %collective-permute-start.1 = (f32[2,16,128]{2,1,0:T(8,128)S(1)}, f32[2,16,128]{2,1,0:T(8,128)S(1)}, u32[]{:S(2)}, u32[]{:S(2)}) collective-permute-start(f32[2,16,128]{2,1,0:T(8,128)S(1)} %get-tuple-element.23.after), channel_id=1, source_target_pairs={{1,0},{2,1},{3,2},{4,3},{5,4},{6,5},{7,6},{0,7},{9,8},{10,9},{11,1... | collective-permute-start | bytes 49160 | tf_op jit(solution)/shard_map/ppermute | solution.py:504
  7.3 4.8 %weigh.1 = (f32[8,5,16,128]{3,2,1,0:T(8,128)}, f32[1280,128]{1,0:T(8,128)S(1)}, f32[8,512]{1,0:T(8,128)S(1)}) custom-call(f32[2,1,256,128]{3,2,1,0:T(8,128)S(1)} %get-tuple-element.24.atm_near, s32[3,1,1,8,64]{4,3,2,1,0:T(8,128)S(1)} %get-tuple-element.25.margins, f32[32,128,128]{2,1,0:T(8,128)} %weights.3, f32[2,16,128]{2,1,0:T(8,128)S(1)} %get-tuple-element.23.after), custom_call_target="tpu_custom_call" | custom-call | flops 4294967296 | bytes 1048576 | tf_op jit(solution)/shard_map/weigh/pallas_call | solution.py:44
  12.1 0.0 collective-permute-done.from_west
  12.1 0.0 collective-permute-done.1.from_east
  12.1 3.4 %all-to-all-start = ((f32[8,5,16,128]{3,2,1,0:T(8,128)}), f32[8,5,16,128]{3,2,1,0:T(8,128)S(1)}, u32[]{:S(2)}, u32[]{:S(2)}) async-start(f32[8,5,16,128]{3,2,1,0:T(8,128)} %get-tuple-element.31), calls=%async_computation | async-start | bytes 655360 | tf_op jit(solution)/shard_map/all_to_all | solution.py:538
  15.6 2.9 %collective-permute-start.2 = (f32[37,8,128]{2,1,0:T(8,128)S(1)}, f32[37,8,128]{2,1,0:T(8,128)S(1)}, u32[]{:S(2)}, u32[]{:S(2)}) collective-permute-start(f32[37,8,128]{2,1,0:T(8,128)S(1)} %get-tuple-element.27), channel_id=1, source_target_pairs={{8,0},{16,8},{24,16},{9,1},{17,9},{25,17},{10,2},{18,10},{26,18},{... | collective-permute-start | bytes 454664 | tf_op jit(solution)/shard_map/ppermute | solution.py:540
  18.5 3.2 %collective-permute-start.3 = (f32[37,8,128]{2,1,0:T(8,128)S(1)}, f32[37,8,128]{2,1,0:T(8,128)S(1)}, u32[]{:S(2)}, u32[]{:S(2)}) collective-permute-start(f32[37,8,128]{2,1,0:T(8,128)S(1)} %get-tuple-element.28), channel_id=1, source_target_pairs={{0,8},{8,16},{16,24},{1,9},{9,17},{17,25},{2,10},{10,18},{18,26},{... | collective-permute-start | bytes 454664 | tf_op jit(solution)/shard_map/ppermute | solution.py:539
  21.7 1.2 %collective-permute-done.2.from_north = f32[37,8,128]{2,1,0:T(8,128)S(1)} collective-permute-done((f32[37,8,128]{2,1,0:T(8,128)S(1)}, f32[37,8,128]{2,1,0:T(8,128)S(1)}, u32[]{:S(2)}, u32[]{:S(2)}) %collective-permute-start.2) | collective-permute-done | bytes 151584 | tf_op jit(solution)/shard_map/ppermute | solution.py:540
  22.9 0.9 %collective-permute-done.3.from_south = f32[37,8,128]{2,1,0:T(8,128)S(1)} collective-permute-done((f32[37,8,128]{2,1,0:T(8,128)S(1)}, f32[37,8,128]{2,1,0:T(8,128)S(1)}, u32[]{:S(2)}, u32[]{:S(2)}) %collective-permute-start.3) | collective-permute-done | bytes 151584 | tf_op jit(solution)/shard_map/ppermute | solution.py:539
  23.8 2.4 %run_adjoint.1 = (f32[2,4,16,256]{3,2,1,0:T(8,128)}, f32[8,64,128]{2,1,0:T(8,128)}, f32[6,4,24,384]{3,2,1,0:T(8,128)S(1)}, f32[2,4,24,384]{3,2,1,0:T(8,128)S(1)}) custom-call(f32[35,16,256]{2,1,0:T(8,128)S(1)} %get-tuple-element.21.fields, f32[2,16,128]{2,1,0:T(8,128)S(1)} %collective-permute-done.from_west, ...), custom_call_target="tpu_custom_call" | custom-call | bytes 1048576 | tf_op jit(solution)/shard_map/run_adjoint/pallas_call | solution.py:44
  26.2 0.0 all-to-all-done.received
  26.2 5.6 %all-to-all-start.1 = ((f32[8,64,128]{2,1,0:T(8,128)}), f32[8,64,128]{2,1,0:T(8,128)S(1)}, u32[]{:S(2)}, u32[]{:S(2)}) async-start(f32[8,64,128]{2,1,0:T(8,128)} %get-tuple-element.36), calls=%async_computation.1 | async-start | bytes 524288 | tf_op jit(solution)/shard_map/all_to_all | solution.py:555
  31.9 0.1 sum_forcing.1
  31.9 1.9 %collective-permute-start.4 = (f32[8,384]{1,0:T(8,128)S(1)}, f32[8,384]{1,0:T(8,128)S(1)}, u32[]{:S(2)}, u32[]{:S(2)}) collective-permute-start(f32[8,384]{1,0:T(8,128)S(1)} %get-tuple-element.33), channel_id=1, source_target_pairs={{8,0},{16,8},{24,16},{9,1},{17,9},{25,17},{10,2},{18,10},{26,18},{... | collective-permute-start | bytes 36872 | tf_op jit(solution)/shard_map/ppermute | solution.py:562
  33.9 4.7 %collective-permute-start.5 = (f32[8,384]{1,0:T(8,128)S(1)}, f32[8,384]{1,0:T(8,128)S(1)}, u32[]{:S(2)}, u32[]{:S(2)}) collective-permute-start(f32[8,384]{1,0:T(8,128)S(1)} %get-tuple-element.34), channel_id=1, source_target_pairs={{0,8},{8,16},{16,24},{1,9},{9,17},{17,25},{2,10},{10,18},{18,26},{... | collective-permute-start | bytes 36872 | tf_op jit(solution)/shard_map/ppermute | solution.py:561
  38.5 0.0 collective-permute-done.4.from_north
  38.5 0.8 %collective-permute-done.5.from_south = f32[8,384]{1,0:T(8,128)S(1)} collective-permute-done((f32[8,384]{1,0:T(8,128)S(1)}, f32[8,384]{1,0:T(8,128)S(1)}, u32[]{:S(2)}, u32[]{:S(2)}) %collective-permute-start.5) | collective-permute-done | bytes 12320 | tf_op jit(solution)/shard_map/ppermute | solution.py:561
  39.3 1.6 %run_forward.1 = f32[2,4,16,256]{3,2,1,0:T(8,128)} custom-call(f32[6,4,24,384]{3,2,1,0:T(8,128)S(1)} %get-tuple-element.29.coeffs, f32[2,4,24,384]{3,2,1,0:T(8,128)S(1)} %get-tuple-element.30.start, f32[2,16,384]{2,1,0:T(8,128)S(1)} %get-tuple-element.32.forcing, f32[8,384]{1,0:T(8,128)S(1)} %collective-permute-done.4.from_north, ...), custom_call_target="tpu_custom_call" | custom-call | bytes 1048576 | tf_op jit(solution)/shard_map/run_forward/pallas_call | solution.py:44
  40.9 0.0 all-to-all-done.1.gathered
  40.9 4.6 %unweigh.1 = f32[2,1,256,128]{3,2,1,0:T(8,128)} custom-call(f32[8,64,128]{2,1,0:T(8,128)S(1)} %all-to-all-done.1.gathered, f32[1280,128]{1,0:T(8,128)S(1)} %get-tuple-element.37.found, f32[8,512]{1,0:T(8,128)S(1)} %get-tuple-element.38.keys, f32[32,128,128]{2,1,0:T(8,128)} %weights.3), custom_call_target="tpu_custom_call" | custom-call | flops 4294967296 | bytes 1048576 | tf_op jit(solution)/shard_map/unweigh/pallas_call | solution.py:44
  (1 shorter events, 0.0 us)
Async XLA Ops:
  2.1 10.0 %collective-permute-start = (f32[2,16,128]{2,1,0:T(8,128)S(1)}, f32[2,16,128]{2,1,0:T(8,128)S(1)}, u32[]{:S(2)}, u32[]{:S(2)}) collective-permute-start(f32[2,16,128]{2,1,0:T(8,128)S(1)} %get-tuple-element.22), channel_id=1, source_target_pairs={{0,1},{1,2},{2,3},{3,4},{4,5},{5,6},{6,7},{7,0},{8,9},{9,10},{10,1... | collective-permute-start | bytes 49160 | tf_op jit(solution)/shard_map/ppermute | solution.py:505
  4.2 7.9 %collective-permute-start.1 = (f32[2,16,128]{2,1,0:T(8,128)S(1)}, f32[2,16,128]{2,1,0:T(8,128)S(1)}, u32[]{:S(2)}, u32[]{:S(2)}) collective-permute-start(f32[2,16,128]{2,1,0:T(8,128)S(1)} %get-tuple-element.23.after), channel_id=1, source_target_pairs={{1,0},{2,1},{3,2},{4,3},{5,4},{6,5},{7,6},{0,7},{9,8},{10,9},{11,1... | collective-permute-start | bytes 49160 | tf_op jit(solution)/shard_map/ppermute | solution.py:504
  12.1 14.1 %all-to-all-start = ((f32[8,5,16,128]{3,2,1,0:T(8,128)}), f32[8,5,16,128]{3,2,1,0:T(8,128)S(1)}, u32[]{:S(2)}, u32[]{:S(2)}) async-start(f32[8,5,16,128]{3,2,1,0:T(8,128)} %get-tuple-element.31), calls=%async_computation | async-start | bytes 655360 | tf_op jit(solution)/shard_map/all_to_all | solution.py:538
  15.6 7.3 %collective-permute-start.2 = (f32[37,8,128]{2,1,0:T(8,128)S(1)}, f32[37,8,128]{2,1,0:T(8,128)S(1)}, u32[]{:S(2)}, u32[]{:S(2)}) collective-permute-start(f32[37,8,128]{2,1,0:T(8,128)S(1)} %get-tuple-element.27), channel_id=1, source_target_pairs={{8,0},{16,8},{24,16},{9,1},{17,9},{25,17},{10,2},{18,10},{26,18},{... | collective-permute-start | bytes 454664 | tf_op jit(solution)/shard_map/ppermute | solution.py:540
  18.5 5.3 %collective-permute-start.3 = (f32[37,8,128]{2,1,0:T(8,128)S(1)}, f32[37,8,128]{2,1,0:T(8,128)S(1)}, u32[]{:S(2)}, u32[]{:S(2)}) collective-permute-start(f32[37,8,128]{2,1,0:T(8,128)S(1)} %get-tuple-element.28), channel_id=1, source_target_pairs={{0,8},{8,16},{16,24},{1,9},{9,17},{17,25},{2,10},{10,18},{18,26},{... | collective-permute-start | bytes 454664 | tf_op jit(solution)/shard_map/ppermute | solution.py:539
  26.2 14.7 %all-to-all-start.1 = ((f32[8,64,128]{2,1,0:T(8,128)}), f32[8,64,128]{2,1,0:T(8,128)S(1)}, u32[]{:S(2)}, u32[]{:S(2)}) async-start(f32[8,64,128]{2,1,0:T(8,128)} %get-tuple-element.36), calls=%async_computation.1 | async-start | bytes 524288 | tf_op jit(solution)/shard_map/all_to_all | solution.py:555
  31.9 6.6 %collective-permute-start.4 = (f32[8,384]{1,0:T(8,128)S(1)}, f32[8,384]{1,0:T(8,128)S(1)}, u32[]{:S(2)}, u32[]{:S(2)}) collective-permute-start(f32[8,384]{1,0:T(8,128)S(1)} %get-tuple-element.33), channel_id=1, source_target_pairs={{8,0},{16,8},{24,16},{9,1},{17,9},{25,17},{10,2},{18,10},{26,18},{... | collective-permute-start | bytes 36872 | tf_op jit(solution)/shard_map/ppermute | solution.py:562
  33.9 5.5 %collective-permute-start.5 = (f32[8,384]{1,0:T(8,128)S(1)}, f32[8,384]{1,0:T(8,128)S(1)}, u32[]{:S(2)}, u32[]{:S(2)}) collective-permute-start(f32[8,384]{1,0:T(8,128)S(1)} %get-tuple-element.34), channel_id=1, source_target_pairs={{0,8},{8,16},{16,24},{1,9},{9,17},{17,25},{2,10},{10,18},{18,26},{... | collective-permute-start | bytes 36872 | tf_op jit(solution)/shard_map/ppermute | solution.py:561
